TPU v7x, 32 devices: a whole 2x2x4 slice. The times are simulated.
32 devices in a mesh: tensor: 16 (over z, x, core), rows: 2 (over y).
Axes of the slice: x: 2, y: 2, z: 4, core: 2. Of those that a mesh axis runs over, the one named last changes fastest.
Arguments:
- image: bfloat16 [16, 64, 3072], P('rows', None, 'tensor'), may hold values from -6 to 6
- dw_kernel: bfloat16 [7, 7, 3072], P(None, None, 'tensor'), may hold values from -0.875 to 0.875
- dw_bias: float32 [3072], P('tensor'), may hold values from -3 to 3
- norm_gain: float32 [3072], replicated, may hold values from 0.1 to 1.9
- norm_bias: float32 [3072], replicated, may hold values from -2 to 2
- w_expand: bfloat16 [3072, 12288], P('rows', 'tensor'), may hold values from -0.15625 to 0.15625
- b_expand: float32 [12288], P('tensor'), may hold values from -3 to 3
- w_project: bfloat16 [12288, 3072], P('tensor', 'rows'), may hold values from -0.078125 to 0.078125
- b_project: float32 [3072], P('tensor'), may hold values from -3 to 3
- layer_scale: float32 [3072], P('tensor'), may hold values from 0.25 to 2
- out_grad: bfloat16 [16, 64, 3072], P('rows', None, 'tensor'), may hold values from -6 to 6
Outputs:
- result: bfloat16 [16, 64, 3072], P('rows', None, 'tensor')
- image_grad: bfloat16 [16, 64, 3072], P('rows', None, 'tensor')
- expand_grad: float32 [3072, 12288], P('rows', 'tensor')
- project_grad: float32 [12288, 3072], P('tensor', 'rows')
- kernel_grad: float32 [7, 7, 3072], P(None, None, 'tensor')
- scale_grad: float32 [3072], P('tensor')
All inputs are finite; a program needn't handle non-finite values.
Results may differ from a plain program's by a relative error of at most 0.022.
Values may be sent and summed in bfloat16 or wider, within the bound.
A program may use at most 128 MiB of HBM per device.

v0:
```python
import math

import jax
import jax.numpy as jnp
from jax import lax
from jax.sharding import PartitionSpec as P

EPSILON = 1e-06


def extended(cells, sides, width):
    for axis, dim in sides:
        count = lax.axis_size(axis)
        ends = count - 1
        head = lax.slice_in_dim(cells, 0, width, axis=dim)
        tail = lax.slice_in_dim(cells, cells.shape[dim] - width, cells.shape[dim], axis=dim)
        cells = jnp.concatenate(
            [
                lax.ppermute(tail, axis, [(i, (i + 1) % count) for i in range(ends)]),
                cells,
                lax.ppermute(head, axis, [((i + 1) % count, i) for i in range(ends)]),
            ],
            axis=dim,
        )
    return cells


def gelu_exact(values):
    return 0.5 * values * (1.0 + lax.erf(values * (1.0 / math.sqrt(2.0))))


def gelu_slope(values):
    cumulative = 0.5 * (1.0 + lax.erf(values * (1.0 / math.sqrt(2.0))))
    density = jnp.exp(-0.5 * values * values) * (1.0 / math.sqrt(2.0 * math.pi))
    return cumulative + values * density


def depthwise(padded, kernel, height, breadth):
    kernel_size = kernel.shape[0]
    summed = jnp.zeros((height, breadth, kernel.shape[2]), jnp.float32)
    for row_shift in range(kernel_size):
        for col_shift in range(kernel_size):
            window = padded[row_shift : row_shift + height, col_shift : col_shift + breadth]
            summed = summed + kernel[row_shift, col_shift].astype(jnp.float32) * window
    return summed


def kernel_terms(padded, gradient, kernel_size):
    height, breadth = (gradient.shape[0], gradient.shape[1])
    kernel_rows = []
    for row_shift in range(kernel_size):
        kernel_line = []
        for col_shift in range(kernel_size):
            window = padded[row_shift : row_shift + height, col_shift : col_shift + breadth]
            kernel_line.append(jnp.sum(window * gradient, axis=(0, 1)))
        kernel_rows.append(jnp.stack(kernel_line))
    return jnp.stack(kernel_rows)


def contract_last(left, right):
    return lax.dot_general(
        left, right, (((1,), (1,)), ((), ())), preferred_element_type=jnp.float32
    )


def contract_first(left, right):
    return lax.dot_general(
        left, right, (((0,), (0,)), ((), ())), preferred_element_type=jnp.float32
    )


def per_device(
    image,
    dw_kernel,
    dw_bias,
    norm_gain,
    norm_bias,
    w_expand,
    b_expand,
    w_project,
    b_project,
    layer_scale,
    out_grad,
):
    kernel_size = dw_kernel.shape[0]
    rim_depth = kernel_size // 2
    height, breadth, channels = image.shape
    positions = height * breadth
    features = norm_gain.shape[0]
    channel_start = lax.axis_index("tensor") * channels
    gain_part = lax.dynamic_slice_in_dim(norm_gain, channel_start, channels)
    shift_part = lax.dynamic_slice_in_dim(norm_bias, channel_start, channels)
    rimmed = extended(image, (("rows", 0),), rim_depth)
    wide_image = jnp.pad(rimmed, ((0, 0), (rim_depth, rim_depth), (0, 0))).astype(jnp.float32)
    convolved = depthwise(wide_image, dw_kernel, height, breadth) + dw_bias
    mixed = convolved.astype(jnp.bfloat16).reshape(positions, channels)
    own_mixed = mixed.astype(jnp.float32)
    plain_sum, square_sum = lax.psum(
        (jnp.sum(own_mixed, 1), jnp.sum(own_mixed * own_mixed, 1)), "tensor"
    )
    average = plain_sum[:, None] / features
    inv_std = lax.rsqrt(square_sum[:, None] / features - average * average + EPSILON)
    centred = (own_mixed - average) * inv_std
    normed_part = (centred * gain_part + shift_part).astype(jnp.bfloat16)
    normed = lax.all_gather(normed_part, "tensor", axis=1, tiled=True)
    columns = normed
    pre = jnp.dot(
        columns,
        lax.all_gather(w_expand, "rows", axis=0, tiled=True),
        preferred_element_type=jnp.float32,
    )
    pre = pre + b_expand
    hidden = gelu_exact(pre).astype(jnp.bfloat16)
    partial_out = jnp.dot(
        hidden,
        lax.all_gather(w_project, "rows", axis=1, tiled=True),
        preferred_element_type=jnp.float32,
    )
    projected = (
        lax.psum_scatter(
            partial_out.astype(jnp.bfloat16), "tensor", scatter_dimension=1, tiled=True
        ).astype(jnp.float32)
        + b_project
    )
    residual = image.reshape(positions, channels).astype(jnp.float32)
    result = (
        (residual + layer_scale * projected).astype(jnp.bfloat16).reshape(height, breadth, channels)
    )
    upstream = out_grad.reshape(positions, channels).astype(jnp.float32)
    scale_term = jnp.sum(upstream * projected, 0)
    scaled_grad = (upstream * layer_scale).astype(jnp.bfloat16)
    grad_panels = lax.all_gather(scaled_grad, "tensor", axis=1, tiled=True)
    project_term = contract_first(hidden, grad_panels)
    project_grad = lax.psum_scatter(
        project_term.astype(jnp.bfloat16), "rows", scatter_dimension=1, tiled=True
    ).astype(jnp.float32)
    columns = grad_panels
    hidden_grad = contract_last(columns, lax.all_gather(w_project, "rows", axis=1, tiled=True))
    pre_grad = (hidden_grad * gelu_slope(pre)).astype(jnp.bfloat16)
    columns = normed
    expand_grad = lax.psum_scatter(
        contract_first(columns, pre_grad).astype(jnp.bfloat16),
        "rows",
        scatter_dimension=0,
        tiled=True,
    ).astype(jnp.float32)
    normed_partial = contract_last(pre_grad, lax.all_gather(w_expand, "rows", axis=0, tiled=True))
    normed_grad = lax.psum_scatter(
        normed_partial.astype(jnp.bfloat16), "tensor", scatter_dimension=1, tiled=True
    ).astype(jnp.float32)
    gain_grad = normed_grad * gain_part
    plain_total, centred_total = lax.psum(
        (jnp.sum(gain_grad, 1), jnp.sum(gain_grad * centred, 1)), "tensor"
    )
    plain_mean = plain_total[:, None] / features
    centred_mean = centred_total[:, None] / features
    mixed_grad = (inv_std * (gain_grad - plain_mean - centred * centred_mean)).astype(jnp.bfloat16)
    mixed_grad = mixed_grad.reshape(height, breadth, channels)
    grad_rimmed = extended(mixed_grad, (("rows", 0),), rim_depth)
    wide_grad = jnp.pad(grad_rimmed, ((0, 0), (rim_depth, rim_depth), (0, 0))).astype(jnp.float32)
    back = depthwise(wide_grad, dw_kernel[::-1, ::-1], height, breadth)
    image_grad = (upstream.reshape(height, breadth, channels) + back).astype(jnp.bfloat16)
    kernel_local = kernel_terms(wide_image, mixed_grad.astype(jnp.float32), kernel_size)
    kernel_grad, scale_grad = lax.psum((kernel_local, scale_term), "rows")
    return (result, image_grad, expand_grad, project_grad, kernel_grad, scale_grad)


def solution(mesh):
    return jax.shard_map(
        per_device,
        mesh=mesh,
        in_specs=(
            P("rows", None, "tensor"),
            P(None, None, "tensor"),
            P("tensor"),
            P(),
            P(),
            P("rows", "tensor"),
            P("tensor"),
            P("tensor", "rows"),
            P("tensor"),
            P("tensor"),
            P("rows", None, "tensor"),
        ),
        out_specs=(
            P("rows", None, "tensor"),
            P("rows", None, "tensor"),
            P("rows", "tensor"),
            P("tensor", "rows"),
            P(None, None, "tensor"),
            P("tensor"),
        ),
        check_vma=False,
    )
```

profile of v0, /device:TPU:0, one launch (start us, length us, event | category | flops | bytes accessed | tf_op | source)
XLA Modules:
  0.0 523.9 jit_solution(14311175737049157714)
XLA Ops:
  7.2 0.7 all-gather.7.cloned.1.call-update
  8.0 0.1 copy-done
  8.1 4.9 collective-permute-start
  13.0 1.3 collective-permute-start.1
  14.4 0.8 dynamic_slice.6
  15.2 0.8 dynamic_slice.7
  16.0 3.6 collective-permute-done.1
  19.5 0.1 fusion.107
  19.7 4.1 convert_reduce_fusion
  24.0 0.1 copy.25
  24.1 32.0 %all-reduce.3 = (f32[512]{0:T(512)S(1)}, f32[512]{0:T(512)S(1)}) all-reduce(f32[512]{0:T(512)S(1)} %reduce_sum.493, f32[512]{0:T(512)S(1)} %reduce_sum.491), channel_id=1, replica_groups=mesh['tensor'=16,'rows'=2] {'tensor'}, use_global_device_ids=true, to_apply=%region_3.4 | all-reduce | flops 1024 | bytes 8192 | tf_op jit(solution)/shard_map/psum | solution.py:98
  56.2 0.8 add_convert_fusion.2
  57.0 0.7 all-gather.9.cloned.1.call-update
  57.8 17.2 %all-gather.7.cloned.1.call-done = bf16[3072,768]{1,0:T(8,128)(2,1)} async-done(((bf16[1536,768]{1,0:T(8,128)(2,1)}), bf16[3072,768]{1,0:T(8,128)(2,1)}) %all-gather.7.cloned.1.call-update) | async-done | bytes 4718608 | tf_op jit(solution)/shard_map/all_gather | solution.py:109
  75.0 48.1 %all-gather.5.cloned.1.call-done = bf16[512,3072]{0,1:T(8,128)(2,1)} async-done(((bf16[512,192]{0,1:T(8,128)(2,1)}), bf16[512,3072]{0,1:T(8,128)(2,1)}) %all-gather.5.cloned.1.call-update) | async-done | bytes 3145744 | tf_op jit(solution)/shard_map/all_gather | solution.py:105
  123.0 7.1 %convolution_add_fusion = f32[512,768]{1,0:T(8,128)} fusion(bf16[512,3072]{0,1:T(8,128)(2,1)} %all-gather.5.cloned.1.call-done, bf16[3072,768]{1,0:T(8,128)(2,1)} %all-gather.7.cloned.1.call-done, f32[768]{0:T(1024)S(1)} %copy-done.6), kind=kOutput, calls=%fused_computation.64 | convolution fusion | flops 2416312320 | bytes 9440256 | tf_op jit(solution)/shard_map/dot_general | solution.py:107
  130.1 55.9 %all-gather.9.cloned.1.call-done = bf16[768,3072]{1,0:T(8,128)(2,1)} async-done(((bf16[768,1536]{1,0:T(8,128)(2,1)}), bf16[768,3072]{1,0:T(8,128)(2,1)}) %all-gather.9.cloned.1.call-update) | async-done | bytes 4718608 | tf_op jit(solution)/shard_map/all_gather | solution.py:116
  186.1 7.2 %convolution_convert_fusion.3 = bf16[512,3072]{0,1:T(8,128)(2,1)} fusion(bf16[768,3072]{1,0:T(8,128)(2,1)} %all-gather.9.cloned.1.call-done, f32[512,768]{1,0:T(8,128)} %convolution_add_fusion), kind=kOutput, calls=%fused_computation.52 | convolution fusion | flops 2419458048 | bytes 9437184 | tf_op jit(solution)/shard_map/dot_general | solution.py:114
  193.3 0.9 copy-done.1
  194.2 0.1 copy.28
  194.4 0.2 copy.26
  194.6 65.1 %reduce-scatter.5.cloned.1.call-done = bf16[512,192]{0,1:T(8,128)(2,1)} async-done(((bf16[512,3072]{0,1:T(8,128)(2,1)}), bf16[512,192]{0,1:T(8,128)(2,1)}) %reduce-scatter.5.cloned.1.call-update) | async-done | bytes 196624 | tf_op jit(solution)/shard_map/reduce_scatter | solution.py:120
  259.7 1.8 multiply_reduce_fusion.1
  261.6 0.2 reduce-scatter.7.cloned.1.call-start
  261.8 44.8 %all-gather.11.cloned.1.call-done = bf16[512,3072]{0,1:T(8,128)(2,1)} async-done(((bf16[512,192]{0,1:T(8,128)(2,1)}), bf16[512,3072]{0,1:T(8,128)(2,1)}) %all-gather.11.cloned.1.call-update) | async-done | bytes 3145744 | tf_op jit(solution)/shard_map/all_gather | solution.py:132
  306.6 6.6 %fusion.5 = bf16[512,768]{1,0:T(8,128)(2,1)S(1)} fusion(f32[512,768]{1,0:T(8,128)} %convolution_add_fusion, bf16[512,3072]{0,1:T(8,128)(2,1)} %all-gather.11.cloned.1.call-done, bf16[768,3072]{1,0:T(8,128)(2,1)} %all-gather.9.cloned.1.call-done), kind=kOutput, calls=%fused_computation.59 | convolution fusion | flops 2419851264 | bytes 10223616 | tf_op jit(solution)/shard_map/dot_general | solution.py:61
  313.2 6.4 %convolution_convert_fusion.2 = bf16[512,3072]{0,1:T(8,128)(2,1)} fusion(bf16[512,768]{1,0:T(8,128)(2,1)S(1)} %fusion.5, bf16[3072,768]{1,0:T(8,128)(2,1)} %all-gather.7.cloned.1.call-done), kind=kOutput, calls=%fused_computation.51 | convolution fusion | flops 2417491968 | bytes 8650752 | tf_op jit(solution)/shard_map/dot_general | solution.py:61
  319.7 6.7 %convolution_convert_fusion.1 = bf16[3072,768]{1,0:T(8,128)(2,1)} fusion(bf16[512,3072]{0,1:T(8,128)(2,1)} %all-gather.5.cloned.1.call-done, bf16[512,768]{1,0:T(8,128)(2,1)S(1)} %fusion.5), kind=kOutput, calls=%fused_computation.50 | convolution fusion | flops 2418278400 | bytes 8650752 | tf_op jit(solution)/shard_map/dot_general | solution.py:67
  326.4 7.3 %convolution_convert_fusion = bf16[768,3072]{1,0:T(8,128)(2,1)} fusion(bf16[512,3072]{0,1:T(8,128)(2,1)} %all-gather.11.cloned.1.call-done, f32[512,768]{1,0:T(8,128)} %convolution_add_fusion), kind=kOutput, calls=%fused_computation.49 | convolution fusion | flops 2420244480 | bytes 9437184 | tf_op jit(solution)/shard_map/dot_general | solution.py:67
  333.8 0.8 copy.27
  334.6 50.2 %reduce-scatter.7.cloned.1.call-done = bf16[512,192]{0,1:T(8,128)(2,1)} async-done(((bf16[512,3072]{0,1:T(8,128)(2,1)}), bf16[512,192]{0,1:T(8,128)(2,1)}) %reduce-scatter.7.cloned.1.call-update) | async-done | bytes 196624 | tf_op jit(solution)/shard_map/reduce_scatter | solution.py:148
  384.8 1.1 fusion.109
  385.9 29.7 %all-reduce.2 = (f32[512]{0:T(512)S(1)}, f32[512]{0:T(512)S(1)}) all-reduce(f32[512]{0:T(512)S(1)} %get-tuple-element.64, f32[512]{0:T(512)S(1)} %get-tuple-element.63), channel_id=1, replica_groups=mesh['tensor'=16,'rows'=2] {'tensor'}, use_global_device_ids=true, to_apply=%region_9.10 | all-reduce | flops 1024 | bytes 8192 | tf_op jit(solution)/shard_map/psum | solution.py:152
  415.6 1.1 multiply_convert_fusion.1
  416.6 0.1 copy.30
  416.9 0.1 copy.29
  417.1 1.3 collective-permute-start.3
  418.4 4.8 collective-permute-start.2
  423.2 0.8 fusion.19
  424.1 1.1 fusion.37
  425.2 1.1 fusion.55
  426.5 9.3 %all-reduce.4 = (f32[7,7,192]{2,1,0:T(8,128)}, f32[192]{0:T(256)}) all-reduce(f32[7,7,192]{2,1,0:T(8,128)S(1)} %constant_dynamic-update-slice_fusion, f32[192]{0:T(256)S(1)} %get-tuple-element.72), channel_id=1, replica_groups=mesh['tensor'=16,'rows'=2] {'rows'}, use_global_device_ids=true, to_apply=%region_61.62 | all-reduce | flops 9600 | bytes 76800 | tf_op jit(solution)/shard_map/psum | solution.py:164
  435.8 0.1 fusion.106
  435.9 4.5 fusion.58
  440.5 9.7 %reduce-scatter.9.cloned.1.call-done = bf16[1536,768]{1,0:T(8,128)(2,1)} async-done(((bf16[3072,768]{1,0:T(8,128)(2,1)}), bf16[1536,768]{1,0:T(8,128)(2,1)}) %reduce-scatter.9.cloned.1.call-update) | async-done | bytes 2359312 | tf_op jit(solution)/shard_map/reduce_scatter | solution.py:141
  450.1 4.2 convert_element_type.304
  454.3 58.2 %reduce-scatter.11.cloned.1.call-done = bf16[768,1536]{1,0:T(8,128)(2,1)} async-done(((bf16[768,3072]{1,0:T(8,128)(2,1)}), bf16[768,1536]{1,0:T(8,128)(2,1)}) %reduce-scatter.11.cloned.1.call-update) | async-done | bytes 2359312 | tf_op jit(solution)/shard_map/reduce_scatter | solution.py:134
  512.5 4.5 convert_element_type.306
  (53 shorter events, 1.1 us)
Async XLA Ops:
  7.2 1.0 copy-start
  7.2 7.1 %copy-start.2 = (bf16[7,7,192]{2,1,0:T(8,128)(2,1)S(1)}, bf16[7,7,192]{2,1,0:T(8,128)(2,1)}, u32[]{:S(2)}) copy-start(bf16[7,7,192]{2,1,0:T(8,128)(2,1)} %param.12) | copy-start | bytes 56452
  7.2 12.5 %copy-start.3 = (f32[192]{0:T(256)S(1)}, f32[192]{0:T(256)}, u32[]{:S(2)}) copy-start(f32[192]{0:T(256)} %param.13) | copy-start | bytes 2308
  7.2 67.8 %all-gather.7.cloned.1.call-start = ((), (), s32[]{:S(2)}) async-start(), calls=%async_computation.5 | async-start | bytes 7077888 | tf_op jit(solution)/shard_map/all_gather | solution.py:109
  7.9 115.1 %all-gather.5.cloned.1.call-start = ((), (), s32[]{:S(2)}) async-start(), calls=%async_computation.4 | async-start | bytes 3342336 | tf_op jit(solution)/shard_map/all_gather | solution.py:105
  8.1 7.8 %collective-permute-start = (bf16[3,64,192]{2,1,0:T(8,128)(2,1)S(1)}, bf16[3,64,192]{2,1,0:T(8,128)(2,1)S(1)}, u32[]{:S(2)}, u32[]{:S(2)}) collective-permute-start(bf16[3,64,192]{2,1,0:T(8,128)(2,1)S(1)} %get-tuple-element.74), channel_id=1, source_target_pairs={{0,1},{2,3},{4,5},{6,7},{8,9},{10,11},{12,13},{14,15},{16,17},{18,... | collective-permute-start | bytes 221192 | tf_op jit(solution)/shard_map/ppermute | solution.py:19
  13.0 6.5 %collective-permute-start.1 = (bf16[3,64,192]{2,1,0:T(8,128)(2,1)S(1)}, bf16[3,64,192]{2,1,0:T(8,128)(2,1)S(1)}, u32[]{:S(2)}, u32[]{:S(2)}) collective-permute-start(bf16[3,64,192]{2,1,0:T(8,128)(2,1)S(1)} %get-tuple-element.75), channel_id=1, source_target_pairs={{1,0},{3,2},{5,4},{7,6},{9,8},{11,10},{13,12},{15,14},{17,16},{19,... | collective-permute-start | bytes 221192 | tf_op jit(solution)/shard_map/ppermute | solution.py:21
  23.8 99.2 %copy-start.6 = (f32[768]{0:T(1024)S(1)}, f32[768]{0:T(1024)}, u32[]{:S(2)}) copy-start(f32[768]{0:T(1024)} %param.17) | copy-start | bytes 9220
  57.0 129.1 %all-gather.9.cloned.1.call-start = ((), (), s32[]{:S(2)}) async-start(), calls=%async_computation.6 | async-start | bytes 7077888 | tf_op jit(solution)/shard_map/all_gather | solution.py:116
  57.7 201.9 %reduce-scatter.5.cloned.1.call-start = ((), (), s32[]{:S(2)}) async-start(), calls=%async_computation.7 | async-start | bytes 3342336 | tf_op jit(solution)/shard_map/reduce_scatter | solution.py:120
  193.3 0.9 copy-start.1
  193.3 66.4 %copy-start.4 = (f32[192]{0:T(256)S(1)}, f32[192]{0:T(256)}, u32[]{:S(2)}) copy-start(f32[192]{0:T(256)} %param.19) | copy-start | bytes 2308
  193.3 66.4 %copy-start.5 = (f32[192]{0:T(256)S(1)}, f32[192]{0:T(256)}, u32[]{:S(2)}) copy-start(f32[192]{0:T(256)} %param.20) | copy-start | bytes 2308
  193.3 113.3 %all-gather.11.cloned.1.call-start = ((), (), s32[]{:S(2)}) async-start(), calls=%async_computation.8 | async-start | bytes 3342336 | tf_op jit(solution)/shard_map/all_gather | solution.py:132
  261.6 123.3 %reduce-scatter.7.cloned.1.call-start = ((), (), s32[]{:S(2)}) async-start(), calls=%async_computation.9 | async-start | bytes 3342336 | tf_op jit(solution)/shard_map/reduce_scatter | solution.py:148
  319.6 130.5 %reduce-scatter.9.cloned.1.call-start = ((), (), s32[]{:S(2)}) async-start(), calls=%async_computation.10 | async-start | bytes 7077888 | tf_op jit(solution)/shard_map/reduce_scatter | solution.py:141
  326.4 186.2 %reduce-scatter.11.cloned.1.call-start = ((), (), s32[]{:S(2)}) async-start(), calls=%async_computation.11 | async-start | bytes 7077888 | tf_op jit(solution)/shard_map/reduce_scatter | solution.py:134
  417.1 18.7 %collective-permute-start.3 = (bf16[3,64,192]{2,1,0:T(8,128)(2,1)S(1)}, bf16[3,64,192]{2,1,0:T(8,128)(2,1)S(1)}, u32[]{:S(2)}, u32[]{:S(2)}) collective-permute-start(bf16[3,64,192]{2,1,0:T(8,128)(2,1)S(1)} %bitcast.187), channel_id=1, source_target_pairs={{1,0},{3,2},{5,4},{7,6},{9,8},{11,10},{13,12},{15,14},{17,16},{19,... | collective-permute-start | bytes 221192 | tf_op jit(solution)/shard_map/ppermute | solution.py:21
  418.4 17.4 %collective-permute-start.2 = (bf16[3,64,192]{2,1,0:T(8,128)(2,1)S(1)}, bf16[3,64,192]{2,1,0:T(8,128)(2,1)S(1)}, u32[]{:S(2)}, u32[]{:S(2)}) collective-permute-start(bf16[3,64,192]{2,1,0:T(8,128)(2,1)S(1)} %bitcast.186), channel_id=1, source_target_pairs={{0,1},{2,3},{4,5},{6,7},{8,9},{10,11},{12,13},{14,15},{16,17},{18,... | collective-permute-start | bytes 221192 | tf_op jit(solution)/shard_map/ppermute | solution.py:19
Sparse Core Ops, SparseCore 0:
  9.6 65.3 all-gather.6
  77.8 45.1 all-gather.4
  124.6 61.4 all-gather.8
  193.4 66.2 reduce-scatter.4
  262.4 44.1 all-gather.10
  319.7 65.0 reduce-scatter.6
  387.7 62.4 reduce-scatter.8
  452.5 59.9 reduce-scatter.10
where the time goes:
time: 524 us
  waiting for transfers between devices  354 us (68%)
  blocking collectives  71 us (14%)
  matrix products  41.3 us (8%)
  other arithmetic  25.6 us (5%)
  between operations  14.4 us (3%)
  starting transfers between devices  12.7 us (2%)
    reduce_scatter x1, waiting for transfers between devices, per_device(): lax.psum_scatter(partial_out.astype(jnp.bfloat16), 'tensor', scatter_dime...  65.1 us
    reduce_scatter x1, waiting for transfers between devices, per_device(): lax.psum_scatter(project_term.astype(jnp.bfloat16), 'rows', scatter_dimen...  58.2 us
    all_gather x1, waiting for transfers between devices, per_device(): lax.all_gather(w_project, 'rows', axis=1, tiled=True)  55.9 us
    reduce_scatter x1, waiting for transfers between devices, per_device(): lax.psum_scatter(normed_partial.astype(jnp.bfloat16), 'tensor', scatter_d...  50.2 us
    all_gather x1, waiting for transfers between devices, per_device(): normed = lax.all_gather(normed_part, 'tensor', axis=1, tiled=True)  48.1 us
    all_gather x1, waiting for transfers between devices, per_device(): grad_panels = lax.all_gather(scaled_grad, 'tensor', axis=1, tiled=True)  44.8 us
    psum x1, blocking collectives, per_device(): lax.psum((jnp.sum(own_mixed, 1), jnp.sum(own_mixed * own_mixed, 1)), 'ten...  32 us
    psum x1, blocking collectives, per_device(): lax.psum((jnp.sum(gain_grad, 1), jnp.sum(gain_grad * centred, 1)), 'tensor')  29.7 us
  transfers between devices with their start and end apart: 12, of which 9 were waited for; matrix products, arithmetic and copies ran while one was open for 8% of the time, Pallas kernels for 0%

commit v1 on v0

--- a/solution.py
+++ b/solution.py
@@ -69,7 +69,7 @@
     )
 
 
-def per_device(
+def general_plan(
     image,
     dw_kernel,
     dw_bias,
@@ -165,9 +165,122 @@
     return (result, image_grad, expand_grad, project_grad, kernel_grad, scale_grad)
 
 
+def pair_swap(value):
+    return lax.ppermute(value, "rows", [(0, 1), (1, 0)])
+
+
+def trade_blocks(block):
+    count = lax.axis_size("tensor")
+    half = count // 2
+    pairs = []
+    for low in range(half):
+        first, second = 2 * low + 1, 2 * (low + half)
+        pairs += [(first, second), (second, first)]
+    other = lax.ppermute(block, ("tensor", "rows"), pairs)
+    upper = lax.axis_index("tensor") >= half
+    stays = upper == (lax.axis_index("rows") == 1)
+    return jnp.where(stays, block, other)
+
+
+def gather_plane(block):
+    count = lax.axis_size("tensor")
+    positions, channels = block.shape
+    gathered = lax.all_gather(trade_blocks(block), "tensor", axis=0)
+    gathered = gathered.reshape(2, count // 2, positions, channels)
+    return gathered.transpose(0, 2, 1, 3).reshape(2 * positions, count // 2 * channels)
+
+
+def scatter_plane(partial):
+    count = lax.axis_size("tensor")
+    positions, channels = partial.shape[0] // 2, partial.shape[1] // (count // 2)
+    blocks = partial.reshape(2, positions, count // 2, channels).transpose(0, 2, 1, 3)
+    blocks = blocks.reshape(count, positions, channels)
+    return trade_blocks(lax.psum_scatter(blocks, "tensor", scatter_dimension=0, tiled=False))
+
+
+def paired_plan(
+    image,
+    dw_kernel,
+    dw_bias,
+    norm_gain,
+    norm_bias,
+    w_expand,
+    b_expand,
+    w_project,
+    b_project,
+    layer_scale,
+    out_grad,
+):
+    kernel_size = dw_kernel.shape[0]
+    rim_depth = kernel_size // 2
+    height, breadth, channels = image.shape
+    positions = height * breadth
+    features = norm_gain.shape[0]
+    half_features = features // 2
+    row = lax.axis_index("rows")
+    channel_start = lax.axis_index("tensor") * channels
+    gain_part = lax.dynamic_slice_in_dim(norm_gain, channel_start, channels)
+    gain_half = lax.dynamic_slice_in_dim(norm_gain, row * half_features, half_features)
+    shift_half = lax.dynamic_slice_in_dim(norm_bias, row * half_features, half_features)
+    upstream = out_grad.reshape(positions, channels).astype(jnp.float32)
+    scaled_grad = (upstream * layer_scale).astype(jnp.bfloat16)
+    grad_panels = gather_plane(scaled_grad)
+    rimmed = extended(image, (("rows", 0),), rim_depth)
+    wide_image = jnp.pad(rimmed, ((0, 0), (rim_depth, rim_depth), (0, 0))).astype(jnp.float32)
+    convolved = depthwise(wide_image, dw_kernel, height, breadth) + dw_bias
+    mixed = convolved.astype(jnp.bfloat16).reshape(positions, channels)
+    mixed_panels = gather_plane(mixed)
+    hidden_partial = contract_last(grad_panels, w_project)
+    hidden_grad = hidden_partial + pair_swap(hidden_partial.astype(jnp.bfloat16))
+    mixed_wide = mixed_panels.astype(jnp.float32)
+    sums = jnp.stack([jnp.sum(mixed_wide, 1), jnp.sum(mixed_wide * mixed_wide, 1)])
+    sums = sums + pair_swap(sums)
+    average = sums[0] / features
+    inv_std = lax.rsqrt(sums[1] / features - average * average + EPSILON)
+    centred_half = (mixed_wide - average[:, None]) * inv_std[:, None]
+    normed = (centred_half * gain_half + shift_half).astype(jnp.bfloat16)
+    pre_partial = jnp.dot(normed, w_expand, preferred_element_type=jnp.float32)
+    pre = pre_partial + pair_swap(pre_partial.astype(jnp.bfloat16)) + b_expand
+    pre_grad = (hidden_grad * gelu_slope(pre)).astype(jnp.bfloat16)
+    normed_partial = contract_last(pre_grad, w_expand)
+    normed_grad = scatter_plane(normed_partial.astype(jnp.bfloat16)).astype(jnp.float32)
+    hidden = gelu_exact(pre).astype(jnp.bfloat16)
+    partial_out = jnp.dot(hidden, w_project, preferred_element_type=jnp.float32)
+    projected = scatter_plane(partial_out.astype(jnp.bfloat16)).astype(jnp.float32) + b_project
+    project_grad = contract_first(hidden, grad_panels)
+    expand_grad = contract_first(normed, pre_grad)
+    residual = image.reshape(positions, channels).astype(jnp.float32)
+    result = (
+        (residual + layer_scale * projected).astype(jnp.bfloat16).reshape(height, breadth, channels)
+    )
+    scale_term = jnp.sum(upstream * projected, 0)
+    own_average = lax.dynamic_slice_in_dim(average, row * positions, positions)[:, None]
+    own_inv_std = lax.dynamic_slice_in_dim(inv_std, row * positions, positions)[:, None]
+    centred = (mixed.astype(jnp.float32) - own_average) * own_inv_std
+    gain_grad = normed_grad * gain_part
+    plain_total, centred_total = lax.psum(
+        (jnp.sum(gain_grad, 1), jnp.sum(gain_grad * centred, 1)), "tensor"
+    )
+    plain_mean = plain_total[:, None] / features
+    centred_mean = centred_total[:, None] / features
+    mixed_grad = (own_inv_std * (gain_grad - plain_mean - centred * centred_mean)).astype(
+        jnp.bfloat16
+    )
+    mixed_grad = mixed_grad.reshape(height, breadth, channels)
+    grad_rimmed = extended(mixed_grad, (("rows", 0),), rim_depth)
+    wide_grad = jnp.pad(grad_rimmed, ((0, 0), (rim_depth, rim_depth), (0, 0))).astype(jnp.float32)
+    back = depthwise(wide_grad, dw_kernel[::-1, ::-1], height, breadth)
+    image_grad = (upstream.reshape(height, breadth, channels) + back).astype(jnp.bfloat16)
+    kernel_local = kernel_terms(wide_image, mixed_grad.astype(jnp.float32), kernel_size)
+    kernel_grad = kernel_local + pair_swap(kernel_local)
+    scale_grad = scale_term + pair_swap(scale_term)
+    return (result, image_grad, expand_grad, project_grad, kernel_grad, scale_grad)
+
+
 def solution(mesh):
+    paired = mesh.shape["rows"] == 2 and mesh.shape["tensor"] % 2 == 0
     return jax.shard_map(
-        per_device,
+        paired_plan if paired else general_plan,
         mesh=mesh,
         in_specs=(
             P("rows", None, "tensor"),

time: 524 us -> 481 us (0.918)
  waiting for transfers between devices: 354 us -> 250 us
  local copies, waits for them, and re-layouts: 4.65 us -> 76.7 us
  blocking collectives: 71 us -> 33.8 us
  starting transfers between devices: 12.7 us -> 38.3 us
  matrix products: 41.3 us -> 28.5 us
  other arithmetic: 25.6 us -> 36.8 us
    all_gather x4 -> x2, waiting for transfers between devices: 166 us -> 75.1 us  [gather_plane(): gathered = lax.all_gather(trade_blocks(block), 'tensor', axis=0)]
    reduce_scatter x4 -> x2, waiting for transfers between devices: 183 us -> 111 us  [scatter_plane(): lax.psum_scatter(blocks, 'tensor', scatter_dimension=0, tiled=False)]
    ppermute x0 -> x9, waiting for transfers between devices: none -> 61.9 us  [the longest x5 61.9 us: pair_swap(): return lax.ppermute(value, 'rows', [(0, 1), (1, 0)])]
    reshape x0 -> x5, local copies, waits for them, and re-layouts: none -> 39.7 us  [the longest x2 18.1 us: scatter_plane(): blocks = blocks.reshape(count, positions, channels)]
    psum x3 -> x1, blocking collectives: 71 us -> 33.8 us  [paired_plan(): lax.psum((jnp.sum(gain_grad, 1), jnp.sum(gain_grad * centred, 1)), 'tensor')]
    convert_element_type x5 -> x3, local copies, waits for them, and re-layouts: 1.4 us -> 19 us  [the longest x1 9.62 us: paired_plan(): mixed_wide = mixed_panels.astype(jnp.float32)]
    ppermute x2, starting transfers between devices: 9.65 us -> 26.1 us  [extended(): lax.ppermute(tail, axis, [(i, (i + 1) % count) for i in range(ends)])]
    ppermute x0 -> x9, starting transfers between devices: none -> 9.29 us  [the longest x5 5.78 us: pair_swap(): return lax.ppermute(value, 'rows', [(0, 1), (1, 0)])]
  transfers between devices with their start and end apart: 12 -> 17, of which waited for: 9 -> 7; matrix products, arithmetic and copies ran while one was open for 8% -> 18% of each run, Pallas kernels for 0% -> 0%
where the time goes in v1:
time: 481 us; the launch traced here: 479 us
  waiting for transfers between devices  250 us (52%)
  local copies, waits for them, and re-layouts  76.7 us (16%)
  starting transfers between devices  38.3 us (8%)
  other arithmetic  36.8 us (8%)
  blocking collectives  33.8 us (7%)
  matrix products  28.5 us (6%)
  between operations  14.7 us (3%)
    reduce_scatter x2, waiting for transfers between devices, scatter_plane(): lax.psum_scatter(blocks, 'tensor', scatter_dimension=0, tiled=False)  111 us
    all_gather x2, waiting for transfers between devices, gather_plane(): gathered = lax.all_gather(trade_blocks(block), 'tensor', axis=0)  75.1 us
    ppermute x5, waiting for transfers between devices, pair_swap(): return lax.ppermute(value, 'rows', [(0, 1), (1, 0)])  61.9 us
    psum x1, blocking collectives, paired_plan(): lax.psum((jnp.sum(gain_grad, 1), jnp.sum(gain_grad * centred, 1)), 'tensor')  33.8 us
    ppermute x2, starting transfers between devices, extended(): lax.ppermute(tail, axis, [(i, (i + 1) % count) for i in range(ends)])  26.1 us
    reshape x2, local copies, waits for them, and re-layouts, scatter_plane(): blocks = blocks.reshape(count, positions, channels)  18.1 us
    dot_general x2, matrix products, contract_first(): lax.dot_general(left, right, (((0,), (0,)), ((), ())), preferred_element_...  13.4 us
    reshape x2, local copies, waits for them, and re-layouts, scatter_plane(): partial.reshape(2, positions, count // 2, channels).transpose(0, 2, 1, 3)  12.5 us
  transfers between devices with their start and end apart: 17, of which 7 were waited for; matrix products, arithmetic and copies ran while one was open for 18% of the time, Pallas kernels for 0%

profile of v1, /device:TPU:0, one launch (start us, length us, event | category | flops | bytes accessed | tf_op | source)
XLA Modules:
  0.0 479.0 jit_solution(14649249733569141856)
XLA Ops:
  7.2 1.2 fusion.108
  9.1 1.8 broadcast_select_fusion.1
  10.9 1.0 fusion.116
  11.9 21.5 %collective-permute-start = (bf16[3,64,192]{2,1,0:T(8,128)(2,1)S(1)}, bf16[3,64,192]{2,1,0:T(8,128)(2,1)S(1)}, u32[]{:S(2)}, u32[]{:S(2)}) collective-permute-start(bf16[3,64,192]{2,1,0:T(8,128)(2,1)S(1)} %get-tuple-element.75), channel_id=1, source_target_pairs={{0,1},{2,3},{4,5},{6,7},{8,9},{10,11},{12,13},{14,15},{16,17},{18,... | collective-permute-start | bytes 221192 | tf_op jit(solution)/shard_map/ppermute | solution.py:19
  33.4 1.3 collective-permute-start.1
  34.7 1.0 slice_convert_fusion.48
  35.7 1.0 slice_convert_fusion.47
  37.8 2.1 collective-permute-done.1
  39.9 1.1 fusion.112
  41.0 4.5 add_convert_fusion.1
  48.9 37.0 %all-gather.7.cloned.1.call-done = bf16[8192,192]{1,0:T(8,128)(2,1)} async-done(((bf16[512,192]{1,0:T(8,128)(2,1)}), bf16[8192,192]{1,0:T(8,128)(2,1)}) %all-gather.7.cloned.1.call-update) | async-done | bytes 3145744 | tf_op jit(solution)/shard_map/all_gather | solution.py:188
  86.0 9.2 %copy.35 = bf16[2,8,512,192]{2,0,3,1:T(2,128)(2,1)} copy(bf16[2,8,512,192]{3,2,1,0:T(8,128)(2,1)} %bitcast.249) | data formatting | bytes 6291456 | tf_op jit(solution)/shard_map/reshape | solution.py:189
  95.1 4.6 copy.44
  99.7 38.1 %all-gather.5.cloned.1.call-done = bf16[8192,192]{1,0:T(8,128)(2,1)} async-done(((bf16[512,192]{1,0:T(8,128)(2,1)}), bf16[8192,192]{1,0:T(8,128)(2,1)}) %all-gather.5.cloned.1.call-update) | async-done | bytes 3145744 | tf_op jit(solution)/shard_map/all_gather | solution.py:188
  137.8 9.6 %copy.31 = f32[2,8,512,192]{2,0,3,1:T(2,128)} copy(bf16[2,8,512,192]{3,2,1,0:T(8,128)(2,1)} %bitcast.250) | data formatting | bytes 9437184 | tf_op jit(solution)/shard_map/convert_element_type | solution.py:235
  147.4 7.1 %bitcast_reduce_fusion = (f32[2,512]{1,0:T(2,128)S(1)}, f32[2,512]{1,0:T(2,128)S(1)}) fusion(f32[2,8,512,192]{2,0,3,1:T(2,128)} %copy.31), kind=kLoop, calls=%fused_computation.49 | loop fusion | flops 4716544 | bytes 6299648 | tf_op jit(solution)/shard_map/reduce_sum | solution.py:236
  154.6 1.5 collective-permute-start.3
  156.1 2.7 fusion.117
  159.4 1.6 copy.41
  161.0 1.5 add_convert_fusion
  162.6 2.8 fusion.118
  165.4 1.5 collective-permute-start.4
  167.0 29.1 %collective-permute-done.7 = bf16[1024,768]{1,0:T(8,128)(2,1)S(1)} collective-permute-done((bf16[1024,768]{1,0:T(8,128)(2,1)S(1)}, bf16[1024,768]{1,0:T(8,128)(2,1)S(1)}, u32[]{:S(2)}, u32[]{:S(2)}) %collective-permute-start.7) | collective-permute-done | bytes 1572896 | tf_op jit(solution)/shard_map/ppermute | solution.py:169
  196.1 32.7 %collective-permute-done.4 = bf16[1024,768]{1,0:T(8,128)(2,1)S(1)} collective-permute-done((bf16[1024,768]{1,0:T(8,128)(2,1)S(1)}, bf16[1024,768]{1,0:T(8,128)(2,1)S(1)}, u32[]{:S(2)}, u32[]{:S(2)}) %collective-permute-start.4) | collective-permute-done | bytes 1572896 | tf_op jit(solution)/shard_map/ppermute | solution.py:169
  228.8 3.0 fusion.6
  231.9 1.1 copy-done.10
  233.0 4.0 convolution_convert_fusion
  237.0 4.6 copy.36
  241.7 6.1 %reshape.101 = bf16[2,512,8,192]{1,0,3,2:T(2,128)(2,1)} reshape(bf16[1024,1536]{0,1:T(8,128)(2,1)} %copy.36) | data formatting | bytes 6291456 | tf_op jit(solution)/shard_map/reshape | solution.py:196
  247.8 9.0 %copy.40 = bf16[2,8,512,192]{3,2,1,0:T(8,128)(2,1)} copy(bf16[2,8,512,192]{2,0,3,1:T(2,128)(2,1)} %bitcast.245) | data formatting | bytes 6291456 | tf_op jit(solution)/shard_map/reshape | solution.py:197
  256.9 1.3 copy-done.9
  258.2 5.6 %convolution_convert_fusion.1 = bf16[1024,1536]{1,0:T(8,128)(2,1)} fusion(bf16[1024,768]{1,0:T(8,128)(2,1)S(1)} %copy-done.9, bf16[768,1536]{1,0:T(8,128)(2,1)} %param.18), kind=kOutput, calls=%fused_computation.55 | convolution fusion | flops 2417491968 | bytes 7077888 | tf_op jit(solution)/shard_map/dot_general | solution.py:248
  263.9 4.8 copy.32
  268.6 6.3 %reshape.96 = bf16[2,512,8,192]{1,0,3,2:T(2,128)(2,1)} reshape(bf16[1024,1536]{0,1:T(8,128)(2,1)} %copy.32) | data formatting | bytes 6291456 | tf_op jit(solution)/shard_map/reshape | solution.py:196
  274.9 9.0 %copy.39 = bf16[2,8,512,192]{3,2,1,0:T(8,128)(2,1)} copy(bf16[2,8,512,192]{2,0,3,1:T(2,128)(2,1)} %bitcast.246) | data formatting | bytes 6291456 | tf_op jit(solution)/shard_map/reshape | solution.py:197
  284.9 42.5 %reduce-scatter.5.cloned.1.call-done = bf16[1,512,192]{2,1,0:T(8,128)(2,1)} async-done(((bf16[16,512,192]{2,1,0:T(8,128)(2,1)}), bf16[1,512,192]{2,1,0:T(8,128)(2,1)}) %reduce-scatter.5.cloned.1.call-update) | async-done | bytes 196624 | tf_op jit(solution)/shard_map/reduce_scatter | solution.py:198
  328.2 7.2 %fusion.119 = f32[1536,768]{1,0:T(8,128)} fusion(bf16[1024,1536]{0,1:T(8,128)(2,1)} %copy-done.7, bf16[1024,768]{1,0:T(8,128)(2,1)} %copy-done.10), kind=kOutput, calls=%fused_computation.308 | convolution fusion | flops 2415919104 | bytes 9437184 | tf_op jit(solution)/shard_map/dot_general | solution.py:67
  335.3 68.6 %reduce-scatter.3.cloned.1.call-done = bf16[1,512,192]{2,1,0:T(8,128)(2,1)} async-done(((bf16[16,512,192]{2,1,0:T(8,128)(2,1)}), bf16[1,512,192]{2,1,0:T(8,128)(2,1)}) %reduce-scatter.3.cloned.1.call-update) | async-done | bytes 196624 | tf_op jit(solution)/shard_map/reduce_scatter | solution.py:198
  403.9 1.3 collective-permute-start.5
  406.5 33.8 %all-reduce.2 = (f32[512]{0:T(512)S(1)}, f32[512]{0:T(512)S(1)}) all-reduce(f32[512]{0:T(512)S(1)} %get-tuple-element.64, f32[512]{0:T(512)S(1)} %get-tuple-element.63), channel_id=1, replica_groups=mesh['tensor'=16,'rows'=2] {'tensor'}, use_global_device_ids=true, to_apply=%region_7.8 | all-reduce | flops 1024 | bytes 8192 | tf_op jit(solution)/shard_map/psum | solution.py:261
  440.3 2.5 fusion.56
  442.8 1.7 fusion.38
  444.5 1.4 fusion.20
  447.0 1.3 collective-permute-start.12
  454.2 1.3 collective-permute-start.10
  455.6 4.6 collective-permute-start.9
  460.2 6.3 %fusion.120 = f32[768,1536]{1,0:T(8,128)} fusion(bf16[1024,768]{1,0:T(8,128)(2,1)S(1)} %copy-done.9, bf16[1024,1536]{0,1:T(8,128)(2,1)} %bitcast.251), kind=kOutput, calls=%fused_computation.309 | convolution fusion | flops 2415919104 | bytes 9437184 | tf_op jit(solution)/shard_map/dot_general | solution.py:67
  467.9 4.6 fusion.59
  (164 shorter events, 16.9 us)
Async XLA Ops:
  7.2 155.4 %copy-start = (bf16[1536,768]{1,0:T(8,128)(2,1)S(1)}, bf16[1536,768]{1,0:T(8,128)(2,1)}, u32[]{:S(2)}) copy-start(bf16[1536,768]{1,0:T(8,128)(2,1)} %param.16) | copy-start | bytes 7077892
  7.2 78.8 %all-gather.7.cloned.1.call-start = ((), (), s32[]{:S(2)}) async-start(), calls=%async_computation.5 | async-start | bytes 4456448 | tf_op jit(solution)/shard_map/all_gather | solution.py:188
  8.4 0.7 collective-permute-start.6
  10.9 126.9 %all-gather.5.cloned.1.call-start = ((), (), s32[]{:S(2)}) async-start(), calls=%async_computation.4 | async-start | bytes 4456448 | tf_op jit(solution)/shard_map/all_gather | solution.py:188
  11.9 25.9 %collective-permute-start = (bf16[3,64,192]{2,1,0:T(8,128)(2,1)S(1)}, bf16[3,64,192]{2,1,0:T(8,128)(2,1)S(1)}, u32[]{:S(2)}, u32[]{:S(2)}) collective-permute-start(bf16[3,64,192]{2,1,0:T(8,128)(2,1)S(1)} %get-tuple-element.75), channel_id=1, source_target_pairs={{0,1},{2,3},{4,5},{6,7},{8,9},{10,11},{12,13},{14,15},{16,17},{18,... | collective-permute-start | bytes 221192 | tf_op jit(solution)/shard_map/ppermute | solution.py:19
  33.4 6.5 %collective-permute-start.1 = (bf16[3,64,192]{2,1,0:T(8,128)(2,1)S(1)}, bf16[3,64,192]{2,1,0:T(8,128)(2,1)S(1)}, u32[]{:S(2)}, u32[]{:S(2)}) collective-permute-start(bf16[3,64,192]{2,1,0:T(8,128)(2,1)S(1)} %get-tuple-element.76), channel_id=1, source_target_pairs={{1,0},{3,2},{5,4},{7,6},{9,8},{11,10},{13,12},{15,14},{17,16},{19,... | collective-permute-start | bytes 221192 | tf_op jit(solution)/shard_map/ppermute | solution.py:21
  36.7 8.8 %copy-start.14 = (f32[1,1,192]{2,1,0:T(1,128)}, f32[1,1,192]{2,1,0:T(1,128)S(1)}, u32[]{:S(2)}) copy-start(f32[1,1,192]{2,1,0:T(1,128)S(1)} %get-tuple-element.111) | copy-start | bytes 2308
  36.7 8.8 %copy-start.16 = (f32[1,1,192]{2,1,0:T(1,128)}, f32[1,1,192]{2,1,0:T(1,128)S(1)}, u32[]{:S(2)}) copy-start(f32[1,1,192]{2,1,0:T(1,128)S(1)} %get-tuple-element.112) | copy-start | bytes 2308
  36.7 8.8 %copy-start.18 = (f32[1,1,192]{2,1,0:T(1,128)}, f32[1,1,192]{2,1,0:T(1,128)S(1)}, u32[]{:S(2)}) copy-start(f32[1,1,192]{2,1,0:T(1,128)S(1)} %get-tuple-element.113) | copy-start | bytes 2308
  36.7 8.8 %copy-start.20 = (f32[1,1,192]{2,1,0:T(1,128)}, f32[1,1,192]{2,1,0:T(1,128)S(1)}, u32[]{:S(2)}) copy-start(f32[1,1,192]{2,1,0:T(1,128)S(1)} %get-tuple-element.114) | copy-start | bytes 2308
  37.6 7.9 %copy-start.22 = (f32[1,1,192]{2,1,0:T(1,128)}, f32[1,1,192]{2,1,0:T(1,128)S(1)}, u32[]{:S(2)}) copy-start(f32[1,1,192]{2,1,0:T(1,128)S(1)} %get-tuple-element.115) | copy-start | bytes 2308
  45.7 0.7 collective-permute-start.2
  47.1 280.2 %reduce-scatter.5.cloned.1.call-start = ((), (), s32[]{:S(2)}) async-start(), calls=%async_computation.3 | async-start | bytes 4456448 | tf_op jit(solution)/shard_map/reduce_scatter | solution.py:198
  147.4 8.7 %copy-start.6 = (bf16[192,8,2,512]{3,1,2,0:T(8,128)(2,1)S(1)}, bf16[192,8,2,512]{3,1,2,0:T(8,128)(2,1)}, u32[]{:S(2)}) copy-start(bf16[192,8,2,512]{3,1,2,0:T(8,128)(2,1)} %copy.44) | copy-start | bytes 9437188
  147.4 8.7 %copy-start.51 = (bf16[768,1536]{1,0:T(8,128)(2,1)S(1)}, bf16[768,1536]{1,0:T(8,128)(2,1)}, u32[]{:S(2)}) copy-start(bf16[768,1536]{1,0:T(8,128)(2,1)} %param.18) | copy-start | bytes 7077892
  154.6 6.4 %collective-permute-start.3 = (f32[2,1024]{1,0:T(2,128)S(1)}, f32[2,1024]{1,0:T(2,128)S(1)}, u32[]{:S(2)}, u32[]{:S(2)}) collective-permute-start(f32[2,1024]{1,0:T(2,128)S(1)} %pad_maximum_fusion), channel_id=1, source_target_pairs={{0,1},{1,0},{2,3},{3,2},{4,5},{5,4},{6,7},{7,6},{8,9},{9,8},{10,11... | collective-permute-start | bytes 24584 | tf_op jit(solution)/shard_map/ppermute | solution.py:169
  158.8 37.3 %collective-permute-start.7 = (bf16[1024,768]{1,0:T(8,128)(2,1)S(1)}, bf16[1024,768]{1,0:T(8,128)(2,1)S(1)}, u32[]{:S(2)}, u32[]{:S(2)}) collective-permute-start(bf16[1024,768]{1,0:T(8,128)(2,1)S(1)} %get-tuple-element.128), channel_id=1, source_target_pairs={{0,1},{1,0},{2,3},{3,2},{4,5},{5,4},{6,7},{7,6},{8,9},{9,8},{10,11... | collective-permute-start | bytes 4718600 | tf_op jit(solution)/shard_map/ppermute | solution.py:169
  162.6 66.2 %copy-start.45 = (f32[768]{0:T(1024)S(1)}, f32[768]{0:T(1024)}, u32[]{:S(2)}) copy-start(f32[768]{0:T(1024)} %param.17) | copy-start | bytes 9220
  165.4 63.4 %collective-permute-start.4 = (bf16[1024,768]{1,0:T(8,128)(2,1)S(1)}, bf16[1024,768]{1,0:T(8,128)(2,1)S(1)}, u32[]{:S(2)}, u32[]{:S(2)}) collective-permute-start(bf16[1024,768]{1,0:T(8,128)(2,1)S(1)} %get-tuple-element.130), channel_id=1, source_target_pairs={{0,1},{1,0},{2,3},{3,2},{4,5},{5,4},{6,7},{7,6},{8,9},{9,8},{10,11... | collective-permute-start | bytes 4718600 | tf_op jit(solution)/shard_map/ppermute | solution.py:169
  256.9 147.1 %reduce-scatter.3.cloned.1.call-start = ((), (), s32[]{:S(2)}) async-start(), calls=%async_computation.2 | async-start | bytes 4456448 | tf_op jit(solution)/shard_map/reduce_scatter | solution.py:198
  327.3 78.7 %copy-start.3 = (bf16[8,64,192]{2,1,0:T(8,128)(2,1)S(1)}, bf16[8,64,192]{2,1,0:T(8,128)(2,1)}, u32[]{:S(2)}) copy-start(bf16[8,64,192]{2,1,0:T(8,128)(2,1)} %copy-done.2) | copy-start | bytes 589828
  327.3 78.7 %copy-start.11 = (bf16[1,512,192]{2,1,0:T(8,128)(2,1)S(1)}, bf16[1,512,192]{2,1,0:T(8,128)(2,1)}, u32[]{:S(2)}) copy-start(bf16[1,512,192]{2,1,0:T(8,128)(2,1)} %reduce-scatter.5.cloned.1.call-done) | copy-start | bytes 589828
  327.3 77.9 %collective-permute-start.8 = (bf16[512,192]{1,0:T(8,128)(2,1)}, bf16[512,192]{1,0:T(8,128)(2,1)S(1)}, u32[]{:S(2)}, u32[]{:S(2)}) collective-permute-start(bf16[512,192]{1,0:T(8,128)(2,1)} %bitcast.253), channel_id=1, source_target_pairs={{1,16},{16,1},{3,18},{18,3},{5,20},{20,5},{7,22},{22,7},{9,24},{24... | collective-permute-start | bytes 589832 | tf_op jit(solution)/shard_map/ppermute | solution.py:179
  403.9 42.1 %collective-permute-start.5 = (bf16[512,192]{1,0:T(8,128)(2,1)}, bf16[512,192]{1,0:T(8,128)(2,1)}, u32[]{:S(2)}, u32[]{:S(2)}) collective-permute-start(bf16[512,192]{1,0:T(8,128)(2,1)} %bitcast.255), channel_id=1, source_target_pairs={{1,16},{16,1},{3,18},{18,3},{5,20},{20,5},{7,22},{22,7},{9,24},{24... | collective-permute-start | bytes 589832 | tf_op jit(solution)/shard_map/ppermute | solution.py:179
  444.5 8.2 %copy-start.46 = (f32[192]{0:T(256)S(1)}, f32[192]{0:T(256)}, u32[]{:S(2)}) copy-start(f32[192]{0:T(256)} %get-tuple-element.15) | copy-start | bytes 2308
  444.5 8.2 %copy-start.47 = (f32[192]{0:T(256)S(1)}, f32[192]{0:T(256)}, u32[]{:S(2)}) copy-start(f32[192]{0:T(256)} %get-tuple-element.16) | copy-start | bytes 2308
  444.5 8.1 %copy-start.48 = (f32[192]{0:T(256)S(1)}, f32[192]{0:T(256)}, u32[]{:S(2)}) copy-start(f32[192]{0:T(256)} %get-tuple-element.17) | copy-start | bytes 2308
  444.5 8.1 %copy-start.49 = (f32[192]{0:T(256)S(1)}, f32[192]{0:T(256)}, u32[]{:S(2)}) copy-start(f32[192]{0:T(256)} %get-tuple-element.18) | copy-start | bytes 2308
  447.0 19.4 %collective-permute-start.12 = (f32[192]{0:T(256)S(1)}, f32[192]{0:T(256)S(1)}, u32[]{:S(2)}, u32[]{:S(2)}) collective-permute-start(f32[192]{0:T(256)S(1)} %get-tuple-element.71), channel_id=1, source_target_pairs={{0,1},{1,0},{2,3},{3,2},{4,5},{5,4},{6,7},{7,6},{8,9},{9,8},{10,11... | collective-permute-start | bytes 2312 | tf_op jit(solution)/shard_map/ppermute | solution.py:169
  453.3 13.7 %collective-permute-start.11 = (f32[7,7,192]{2,1,0:T(8,128)S(1)}, f32[7,7,192]{2,1,0:T(8,128)S(1)}, u32[]{:S(2)}, u32[]{:S(2)}) collective-permute-start(f32[7,7,192]{2,1,0:T(8,128)S(1)} %constant_dynamic-update-slice_fusion), channel_id=1, source_target_pairs={{0,1},{1,0},{2,3},{3,2},{4,5},{5,4},{6,7},{7,6},{8,9},{9,8},{10,11... | collective-permute-start | bytes 112904 | tf_op jit(solution)/shard_map/ppermute | solution.py:169
  454.2 13.5 %collective-permute-start.10 = (bf16[3,64,192]{2,1,0:T(8,128)(2,1)S(1)}, bf16[3,64,192]{2,1,0:T(8,128)(2,1)S(1)}, u32[]{:S(2)}, u32[]{:S(2)}) collective-permute-start(bf16[3,64,192]{2,1,0:T(8,128)(2,1)S(1)} %bitcast.257), channel_id=1, source_target_pairs={{1,0},{3,2},{5,4},{7,6},{9,8},{11,10},{13,12},{15,14},{17,16},{19,... | collective-permute-start | bytes 221192 | tf_op jit(solution)/shard_map/ppermute | solution.py:21
  455.4 12.3 %copy-start.5 = (bf16[8,64,192]{2,1,0:T(8,128)(2,1)S(1)}, bf16[8,64,192]{2,1,0:T(8,128)(2,1)}, u32[]{:S(2)}) copy-start(bf16[8,64,192]{2,1,0:T(8,128)(2,1)} %param.21) | copy-start | bytes 589828
  455.5 12.3 %copy-start.15 = (f32[1,1,192]{2,1,0:T(1,128)S(1)}, f32[1,1,192]{2,1,0:T(1,128)}, u32[]{:S(2)}) copy-start(f32[1,1,192]{2,1,0:T(1,128)} %copy-done.14) | copy-start | bytes 2308
  455.5 12.3 %copy-start.17 = (f32[1,1,192]{2,1,0:T(1,128)S(1)}, f32[1,1,192]{2,1,0:T(1,128)}, u32[]{:S(2)}) copy-start(f32[1,1,192]{2,1,0:T(1,128)} %copy-done.16) | copy-start | bytes 2308
  455.5 12.3 %copy-start.19 = (f32[1,1,192]{2,1,0:T(1,128)S(1)}, f32[1,1,192]{2,1,0:T(1,128)}, u32[]{:S(2)}) copy-start(f32[1,1,192]{2,1,0:T(1,128)} %copy-done.18) | copy-start | bytes 2308
  455.5 12.3 %copy-start.21 = (f32[1,1,192]{2,1,0:T(1,128)S(1)}, f32[1,1,192]{2,1,0:T(1,128)}, u32[]{:S(2)}) copy-start(f32[1,1,192]{2,1,0:T(1,128)} %copy-done.20) | copy-start | bytes 2308
  455.5 12.3 %copy-start.23 = (f32[1,1,192]{2,1,0:T(1,128)S(1)}, f32[1,1,192]{2,1,0:T(1,128)}, u32[]{:S(2)}) copy-start(f32[1,1,192]{2,1,0:T(1,128)} %copy-done.22) | copy-start | bytes 2308
  455.5 12.3 %copy-start.25 = (f32[1,1,192]{2,1,0:T(1,128)S(1)}, f32[1,1,192]{2,1,0:T(1,128)}, u32[]{:S(2)}) copy-start(f32[1,1,192]{2,1,0:T(1,128)} %copy-done.24) | copy-start | bytes 2308
  455.5 12.3 %copy-start.27 = (f32[1,1,192]{2,1,0:T(1,128)S(1)}, f32[1,1,192]{2,1,0:T(1,128)}, u32[]{:S(2)}) copy-start(f32[1,1,192]{2,1,0:T(1,128)} %copy-done.26) | copy-start | bytes 2308
  455.5 12.3 %copy-start.29 = (f32[1,1,192]{2,1,0:T(1,128)S(1)}, f32[1,1,192]{2,1,0:T(1,128)}, u32[]{:S(2)}) copy-start(f32[1,1,192]{2,1,0:T(1,128)} %copy-done.28) | copy-start | bytes 2308
  455.5 12.3 %copy-start.31 = (f32[1,1,192]{2,1,0:T(1,128)S(1)}, f32[1,1,192]{2,1,0:T(1,128)}, u32[]{:S(2)}) copy-start(f32[1,1,192]{2,1,0:T(1,128)} %copy-done.30) | copy-start | bytes 2308
  455.5 12.3 %copy-start.33 = (f32[1,1,192]{2,1,0:T(1,128)S(1)}, f32[1,1,192]{2,1,0:T(1,128)}, u32[]{:S(2)}) copy-start(f32[1,1,192]{2,1,0:T(1,128)} %copy-done.32) | copy-start | bytes 2308
  455.6 12.3 %copy-start.35 = (f32[1,1,192]{2,1,0:T(1,128)S(1)}, f32[1,1,192]{2,1,0:T(1,128)}, u32[]{:S(2)}) copy-start(f32[1,1,192]{2,1,0:T(1,128)} %copy-done.34) | copy-start | bytes 2308
  455.6 12.3 %copy-start.37 = (f32[1,1,192]{2,1,0:T(1,128)S(1)}, f32[1,1,192]{2,1,0:T(1,128)}, u32[]{:S(2)}) copy-start(f32[1,1,192]{2,1,0:T(1,128)} %copy-done.36) | copy-start | bytes 2308
  455.6 12.3 %copy-start.39 = (f32[1,1,192]{2,1,0:T(1,128)S(1)}, f32[1,1,192]{2,1,0:T(1,128)}, u32[]{:S(2)}) copy-start(f32[1,1,192]{2,1,0:T(1,128)} %copy-done.38) | copy-start | bytes 2308
  455.6 12.3 %copy-start.41 = (f32[1,1,192]{2,1,0:T(1,128)S(1)}, f32[1,1,192]{2,1,0:T(1,128)}, u32[]{:S(2)}) copy-start(f32[1,1,192]{2,1,0:T(1,128)} %copy-done.40) | copy-start | bytes 2308
  455.6 12.3 %copy-start.43 = (f32[1,1,192]{2,1,0:T(1,128)S(1)}, f32[1,1,192]{2,1,0:T(1,128)}, u32[]{:S(2)}) copy-start(f32[1,1,192]{2,1,0:T(1,128)} %copy-done.42) | copy-start | bytes 2308
  455.6 12.0 %collective-permute-start.9 = (bf16[3,64,192]{2,1,0:T(8,128)(2,1)S(1)}, bf16[3,64,192]{2,1,0:T(8,128)(2,1)S(1)}, u32[]{:S(2)}, u32[]{:S(2)}) collective-permute-start(bf16[3,64,192]{2,1,0:T(8,128)(2,1)S(1)} %bitcast.256), channel_id=1, source_target_pairs={{0,1},{2,3},{4,5},{6,7},{8,9},{10,11},{12,13},{14,15},{16,17},{18,... | collective-permute-start | bytes 221192 | tf_op jit(solution)/shard_map/ppermute | solution.py:19
  (23 other events, 104.6 us)
Sparse Core Ops, SparseCore 0:
  11.0 74.9 all-gather.6
  88.7 49.0 all-gather.4
  257.0 70.3 reduce-scatter.4
  332.1 71.7 reduce-scatter.2

commit v2 on v1

--- a/solution.py
+++ b/solution.py
@@ -1,8 +1,11 @@
+import functools
 import math
 
 import jax
 import jax.numpy as jnp
 from jax import lax
+from jax.experimental import pallas as pl
+from jax.experimental.pallas import tpu as pltpu
 from jax.sharding import PartitionSpec as P
 
 EPSILON = 1e-06
@@ -169,33 +172,299 @@
     return lax.ppermute(value, "rows", [(0, 1), (1, 0)])
 
 
-def trade_blocks(block):
-    count = lax.axis_size("tensor")
-    half = count // 2
-    pairs = []
-    for low in range(half):
-        first, second = 2 * low + 1, 2 * (low + half)
-        pairs += [(first, second), (second, first)]
-    other = lax.ppermute(block, ("tensor", "rows"), pairs)
-    upper = lax.axis_index("tensor") >= half
-    stays = upper == (lax.axis_index("rows") == 1)
-    return jnp.where(stays, block, other)
-
-
-def gather_plane(block):
+MESH = pl.DeviceIdType.MESH
+CHIP_STEPS = (2, 1, 3)
+
+
+class Place:
+    def __init__(self):
+        self.tensor = lax.axis_index("tensor")
+        self.row = lax.axis_index("rows")
+        self.core = lax.rem(self.tensor, 2)
+        self.column = lax.rem(self.tensor // 2, 2)
+        self.count = lax.axis_size("tensor")
+        self.across = self.tensor + 2 - 4 * self.column
+        self.sibling = self.tensor + 1 - 2 * self.core
+        self.traded = (self.tensor // (self.count // 2)) != self.row
+        self.trader = lax.rem(self.tensor + self.count // 2, self.count)
+
+    def along(self, step):
+        return lax.rem(self.tensor + 4 * step, self.count)
+
+    def here(self, tensor):
+        return (tensor, self.row)
+
+    def meet(self):
+        barrier = pltpu.get_barrier_semaphore()
+        peers = [self.sibling, self.across] + [self.along(step) for step in CHIP_STEPS]
+        for peer in peers:
+            pl.semaphore_signal(barrier, inc=1, device_id=self.here(peer), device_id_type=MESH)
+
+        pl.semaphore_signal(
+            barrier, inc=1, device_id=(self.trader, 1 - self.row), device_id_type=MESH
+        )
+        pl.semaphore_wait(barrier, len(peers) + 1)
+
+
+def remote(source, target, sems, device):
+    return pltpu.make_async_remote_copy(
+        src_ref=source,
+        dst_ref=target,
+        send_sem=sems.at[0],
+        recv_sem=sems.at[1],
+        device_id=device,
+        device_id_type=MESH,
+    )
+
+
+def region(ref, tensor, core, quarter, width, count):
+    half = tensor // (count // 2)
+    panel = lax.rem(tensor, count // 2) // 2
+    rows = pl.ds(pl.multiple_of(half * 2 * quarter + core * quarter, quarter), quarter)
+    return ref.at[rows, pl.ds(pl.multiple_of(panel * width, 128), width)]
+
+
+def gather_kernel(block_ref, out_ref, arrived, block, pre_sem, swap_sem, z_sem, x_sem, c_sem):
+    place = Place()
+    quarter = block_ref.shape[0] // 2
+    width = block.shape[1]
+
+    def spot(tensor):
+        return region(out_ref, tensor, place.core, quarter, width, place.count)
+
+    place.meet()
+    other_rows = pl.ds(pl.multiple_of((1 - place.core) * quarter, quarter), quarter)
+    own_rows = pl.ds(pl.multiple_of(place.core * quarter, quarter), quarter)
+    pairing = remote(block_ref.at[other_rows, :], arrived, pre_sem, place.here(place.sibling))
+    pairing.start()
+    pairing.wait()
+
+    @pl.when(place.core == 0)
+    def _():
+        block[...] = jnp.concatenate([block_ref[own_rows, :], arrived[...]], axis=1)
+
+    @pl.when(place.core == 1)
+    def _():
+        block[...] = jnp.concatenate([arrived[...], block_ref[own_rows, :]], axis=1)
+
+    @pl.when(place.traded)
+    def _():
+        swap = remote(block, spot(place.trader), swap_sem, (place.trader, 1 - place.row))
+        swap.start()
+        swap.wait()
+
+    @pl.when(jnp.logical_not(place.traded))
+    def _():
+        keep = pltpu.make_async_copy(block, spot(place.tensor), swap_sem.at[0])
+        keep.start()
+        keep.wait()
+
+    mine = spot(place.tensor)
+    z_copies = [
+        remote(mine, mine, z_sem.at[step], place.here(place.along(step))) for step in CHIP_STEPS
+    ]
+    for copy in z_copies:
+        copy.start()
+    x_copies, c_copies = [], []
+    for index, step in enumerate((0,) + CHIP_STEPS):
+        if step:
+            z_copies[index - 1].wait_recv()
+        origin = lax.rem(place.tensor + 4 * (4 - step), place.count)
+        chunk = spot(origin)
+        x_copies.append(remote(chunk, chunk, x_sem.at[index], place.here(place.across)))
+        c_copies.append(remote(chunk, chunk, c_sem.at[index], place.here(place.sibling)))
+        x_copies[-1].start()
+        c_copies[-1].start()
+    for index, step in enumerate((0,) + CHIP_STEPS):
+        x_copies[index].wait_recv()
+        origin = lax.rem(place.across + 4 * (4 - step), place.count)
+        chunk = spot(origin)
+        c_copies.append(remote(chunk, chunk, c_sem.at[4 + index], place.here(place.sibling)))
+        c_copies[-1].start()
+    for copy in c_copies:
+        copy.wait_recv()
+    for copy in z_copies + x_copies + c_copies:
+        copy.wait_send()
+
+
+def gather_plane(block, collective_id):
     count = lax.axis_size("tensor")
     positions, channels = block.shape
-    gathered = lax.all_gather(trade_blocks(block), "tensor", axis=0)
-    gathered = gathered.reshape(2, count // 2, positions, channels)
-    return gathered.transpose(0, 2, 1, 3).reshape(2 * positions, count // 2 * channels)
-
-
-def scatter_plane(partial):
+    quarter, width = positions // 2, 2 * channels
+    dma = pltpu.SemaphoreType.DMA
+    return pl.pallas_call(
+        gather_kernel,
+        out_shape=jax.ShapeDtypeStruct((2 * positions, count // 2 * channels), block.dtype),
+        in_specs=[pl.BlockSpec(memory_space=pltpu.VMEM)],
+        out_specs=pl.BlockSpec(memory_space=pltpu.VMEM),
+        scratch_shapes=[
+            pltpu.VMEM((quarter, channels), block.dtype),
+            pltpu.VMEM((quarter, width), block.dtype),
+            dma((2,)),
+            dma((2,)),
+            dma((4, 2)),
+            dma((4, 2)),
+            dma((8, 2)),
+        ],
+        compiler_params=pltpu.CompilerParams(
+            collective_id=collective_id, has_side_effects=True, vmem_limit_bytes=24 * 2**20
+        ),
+        name="gather_plane",
+    )(block)
+
+
+def scatter_kernel(arrays, *refs):
+    partials, outs = refs[:arrays], refs[arrays : 2 * arrays]
+    from_core, to_x, from_x, to_z, from_z, kept, final, swapped, leaving = refs[
+        2 * arrays : 2 * arrays + 9
+    ]
+    c_sem, x_sem, z_sem, swap_sem, end_sem = refs[2 * arrays + 9 :]
+    place = Place()
+    quarter, width = final.shape[1:]
+    channels = width // 2
+    place.meet()
+    copies = []
+    c_copies = []
+    for a in range(arrays):
+        for half in range(2):
+            start = half * 2 * quarter + (1 - place.core) * quarter
+            rows = pl.ds(pl.multiple_of(start, quarter), quarter)
+            copy = remote(
+                partials[a].at[rows, :],
+                from_core.at[a, half],
+                c_sem.at[a, half],
+                place.here(place.sibling),
+            )
+            copy.start()
+            c_copies.append(copy)
+
+    def chip_sum(a, tensor):
+        half = tensor // (place.count // 2)
+        panel = lax.rem(tensor, place.count // 2) // 2
+        lanes = pl.ds(pl.multiple_of(panel * width, 128), width)
+        start = half * 2 * quarter + place.core * quarter
+        rows = pl.ds(pl.multiple_of(start, quarter), quarter)
+        own = partials[a][rows, lanes].astype(jnp.float32)
+        return own + from_core[a, half, :, lanes].astype(jnp.float32)
+
+    x_copies, z_copies = {}, {}
+    for a in range(arrays):
+        c_copies[2 * a].wait_recv()
+        c_copies[2 * a + 1].wait_recv()
+        for step in CHIP_STEPS + (0,):
+            target = lax.rem(place.across + 4 * step, place.count)
+            to_x[a, step] = chip_sum(a, target).astype(to_x.dtype)
+            copy = remote(
+                to_x.at[a, step], from_x.at[a, step], x_sem.at[a, step], place.here(place.across)
+            )
+            copy.start()
+            x_copies[a, step] = copy
+    for a in range(arrays):
+        for step in CHIP_STEPS + (0,):
+            target = place.along(step)
+            x_copies[a, step].wait_recv()
+            summed = chip_sum(a, target) + from_x[a, step].astype(jnp.float32)
+            if step:
+                to_z[a, step] = summed.astype(to_z.dtype)
+                copy = remote(
+                    to_z.at[a, step], from_z.at[a, step], z_sem.at[a, step], place.here(target)
+                )
+                copy.start()
+                z_copies[a, step] = copy
+            else:
+                kept[a] = summed
+    swaps = []
+    for a in range(arrays):
+        summed = kept[a]
+        for step in CHIP_STEPS:
+            z_copies[a, step].wait_recv()
+            summed = summed + from_z[a, step].astype(jnp.float32)
+        final[a] = summed.astype(final.dtype)
+        swap = remote(
+            final.at[a], swapped.at[a], swap_sem.at[a], (place.trader, 1 - place.row)
+        )
+        swaps.append(swap)
+
+        @pl.when(place.traded)
+        def _():
+            swap.start()
+
+    ends = []
+    own_rows = pl.ds(pl.multiple_of(place.core * quarter, quarter), quarter)
+    for a in range(arrays):
+
+        @pl.when(place.traded)
+        def _():
+            swaps[a].wait()
+
+        @pl.when(jnp.logical_not(place.traded))
+        def _():
+            swapped[a] = final[a]
+
+        @pl.when(place.core == 0)
+        def _():
+            outs[a][own_rows, :] = swapped[a][:, :channels]
+            leaving[a] = swapped[a][:, channels:]
+
+        @pl.when(place.core == 1)
+        def _():
+            outs[a][own_rows, :] = swapped[a][:, channels:]
+            leaving[a] = swapped[a][:, :channels]
+
+        copy = remote(
+            leaving.at[a], outs[a].at[own_rows, :], end_sem.at[a], place.here(place.sibling)
+        )
+        copy.start()
+        ends.append(copy)
+    for copy in ends:
+        copy.wait()
+    for copy in c_copies + list(x_copies.values()) + list(z_copies.values()):
+        copy.wait_send()
+
+
+def scatter_plane(partials, collective_id):
     count = lax.axis_size("tensor")
-    positions, channels = partial.shape[0] // 2, partial.shape[1] // (count // 2)
-    blocks = partial.reshape(2, positions, count // 2, channels).transpose(0, 2, 1, 3)
-    blocks = blocks.reshape(count, positions, channels)
-    return trade_blocks(lax.psum_scatter(blocks, "tensor", scatter_dimension=0, tiled=False))
+    arrays = len(partials)
+    positions, channels = partials[0].shape[0] // 2, partials[0].shape[1] // (count // 2)
+    quarter, width = positions // 2, 2 * channels
+    dma = pltpu.SemaphoreType.DMA
+    kind = partials[0].dtype
+    vmem = pl.BlockSpec(memory_space=pltpu.VMEM)
+    return pl.pallas_call(
+        functools.partial(scatter_kernel, arrays),
+        out_shape=[jax.ShapeDtypeStruct((positions, channels), kind)] * arrays,
+        in_specs=[vmem] * arrays,
+        out_specs=[vmem] * arrays,
+        scratch_shapes=[
+            pltpu.VMEM((arrays, 2, quarter, partials[0].shape[1]), kind),
+            pltpu.VMEM((arrays, 4, quarter, width), kind),
+            pltpu.VMEM((arrays, 4, quarter, width), kind),
+            pltpu.VMEM((arrays, 4, quarter, width), kind),
+            pltpu.VMEM((arrays, 4, quarter, width), kind),
+            pltpu.VMEM((arrays, quarter, width), jnp.float32),
+            pltpu.VMEM((arrays, quarter, width), kind),
+            pltpu.VMEM((arrays, quarter, width), kind),
+            pltpu.VMEM((arrays, quarter, channels), kind),
+            dma((arrays, 2, 2)),
+            dma((arrays, 4, 2)),
+            dma((arrays, 4, 2)),
+            dma((arrays, 2)),
+            dma((arrays, 2)),
+        ],
+        compiler_params=pltpu.CompilerParams(
+            collective_id=collective_id, has_side_effects=True, vmem_limit_bytes=40 * 2**20
+        ),
+        name="scatter_plane",
+    )(*partials)
+
+
+def butterfly(values):
+    count = lax.axis_size("tensor")
+    step = 1
+    while step < count:
+        values = values + lax.ppermute(values, "tensor", [(i, i ^ step) for i in range(count)])
+        step *= 2
+    return values
 
 
 def paired_plan(
@@ -224,12 +493,12 @@
     shift_half = lax.dynamic_slice_in_dim(norm_bias, row * half_features, half_features)
     upstream = out_grad.reshape(positions, channels).astype(jnp.float32)
     scaled_grad = (upstream * layer_scale).astype(jnp.bfloat16)
-    grad_panels = gather_plane(scaled_grad)
+    grad_panels = gather_plane(scaled_grad, 0)
     rimmed = extended(image, (("rows", 0),), rim_depth)
     wide_image = jnp.pad(rimmed, ((0, 0), (rim_depth, rim_depth), (0, 0))).astype(jnp.float32)
     convolved = depthwise(wide_image, dw_kernel, height, breadth) + dw_bias
     mixed = convolved.astype(jnp.bfloat16).reshape(positions, channels)
-    mixed_panels = gather_plane(mixed)
+    mixed_panels = gather_plane(mixed, 1)
     hidden_partial = contract_last(grad_panels, w_project)
     hidden_grad = hidden_partial + pair_swap(hidden_partial.astype(jnp.bfloat16))
     mixed_wide = mixed_panels.astype(jnp.float32)
@@ -243,10 +512,13 @@
     pre = pre_partial + pair_swap(pre_partial.astype(jnp.bfloat16)) + b_expand
     pre_grad = (hidden_grad * gelu_slope(pre)).astype(jnp.bfloat16)
     normed_partial = contract_last(pre_grad, w_expand)
-    normed_grad = scatter_plane(normed_partial.astype(jnp.bfloat16)).astype(jnp.float32)
     hidden = gelu_exact(pre).astype(jnp.bfloat16)
     partial_out = jnp.dot(hidden, w_project, preferred_element_type=jnp.float32)
-    projected = scatter_plane(partial_out.astype(jnp.bfloat16)).astype(jnp.float32) + b_project
+    normed_block, projected_block = scatter_plane(
+        [normed_partial.astype(jnp.bfloat16), partial_out.astype(jnp.bfloat16)], 2
+    )
+    normed_grad = normed_block.astype(jnp.float32)
+    projected = projected_block.astype(jnp.float32) + b_project
     project_grad = contract_first(hidden, grad_panels)
     expand_grad = contract_first(normed, pre_grad)
     residual = image.reshape(positions, channels).astype(jnp.float32)
@@ -258,11 +530,9 @@
     own_inv_std = lax.dynamic_slice_in_dim(inv_std, row * positions, positions)[:, None]
     centred = (mixed.astype(jnp.float32) - own_average) * own_inv_std
     gain_grad = normed_grad * gain_part
-    plain_total, centred_total = lax.psum(
-        (jnp.sum(gain_grad, 1), jnp.sum(gain_grad * centred, 1)), "tensor"
-    )
-    plain_mean = plain_total[:, None] / features
-    centred_mean = centred_total[:, None] / features
+    totals = butterfly(jnp.stack([jnp.sum(gain_grad, 1), jnp.sum(gain_grad * centred, 1)]))
+    plain_mean = totals[0][:, None] / features
+    centred_mean = totals[1][:, None] / features
     mixed_grad = (own_inv_std * (gain_grad - plain_mean - centred * centred_mean)).astype(
         jnp.bfloat16
     )
@@ -278,7 +548,7 @@
 
 
 def solution(mesh):
-    paired = mesh.shape["rows"] == 2 and mesh.shape["tensor"] % 2 == 0
+    paired = mesh.shape["rows"] == 2 and mesh.shape["tensor"] == 16
     return jax.shard_map(
         paired_plan if paired else general_plan,
         mesh=mesh,

time: 481 us -> 298 us (0.62)
  waiting for transfers between devices: 250 us -> 65.1 us
  Pallas kernels: 0 us -> 135 us
  local copies, waits for them, and re-layouts: 76.7 us -> 3.48 us
  blocking collectives: 33.8 us -> 0 us
  between operations: 14.7 us -> 1.32 us
  other arithmetic: 36.8 us -> 25.9 us
    pallas_call x0 -> x3, Pallas kernels: none -> 135 us  [the longest x2 82.3 us: gather_plane(): pl.pallas_call(gather_kernel, out_shape=jax.ShapeDtypeStruct((2 * positio...]
    reduce_scatter x2 -> x0, waiting for transfers between devices: 111 us -> none  [scatter_plane(): lax.psum_scatter(blocks, 'tensor', scatter_dimension=0, tiled=False)]
    all_gather x2 -> x0, waiting for transfers between devices: 75.1 us -> none  [gather_plane(): gathered = lax.all_gather(trade_blocks(block), 'tensor', axis=0)]
    reshape x5 -> x0, local copies, waits for them, and re-layouts: 39.7 us -> none  [the longest x2 18.1 us: scatter_plane(): blocks = blocks.reshape(count, positions, channels)]
    psum x1 -> x0, blocking collectives: 33.8 us -> none  [paired_plan(): lax.psum((jnp.sum(gain_grad, 1), jnp.sum(gain_grad * centred, 1)), 'tensor')]
    convert_element_type x3 -> x0, local copies, waits for them, and re-layouts: 19 us -> none  [the longest x1 9.62 us: paired_plan(): mixed_wide = mixed_panels.astype(jnp.float32)]
    ppermute x4, starting transfers between devices: 3.5 us -> 20.5 us  [butterfly(): lax.ppermute(values, 'tensor', [(i, i ^ step) for i in range(count)])]
    ppermute x2, starting transfers between devices: 26.1 us -> 9.43 us  [extended(): lax.ppermute(tail, axis, [(i, (i + 1) % count) for i in range(ends)])]
  transfers between devices with their start and end apart: 17 -> 13, of which waited for: 7 -> 5; matrix products, arithmetic and copies ran while one was open for 18% -> 12% of each run, Pallas kernels for 0% -> 14%
where the time goes in v2:
time: 298 us
  Pallas kernels  135 us (45%)
  waiting for transfers between devices  65.1 us (22%)
  starting transfers between devices  36.6 us (12%)
  matrix products  30 us (10%)
  other arithmetic  25.9 us (9%)
  local copies, waits for them, and re-layouts  3.48 us (1%)
    pallas_call x2, Pallas kernels, gather_plane(): pl.pallas_call(gather_kernel, out_shape=jax.ShapeDtypeStruct((2 * positio...  82.3 us
    ppermute x5, waiting for transfers between devices, pair_swap(): return lax.ppermute(value, 'rows', [(0, 1), (1, 0)])  60.6 us
    pallas_call x1, Pallas kernels, scatter_plane(): pl.pallas_call(functools.partial(scatter_kernel, arrays), out_shape=[jax....  52.8 us
    ppermute x4, starting transfers between devices, butterfly(): lax.ppermute(values, 'tensor', [(i, i ^ step) for i in range(count)])  20.5 us
    dot_general x2, matrix products, contract_first(): lax.dot_general(left, right, (((0,), (0,)), ((), ())), preferred_element_...  12.2 us
    ppermute x2, starting transfers between devices, extended(): lax.ppermute(tail, axis, [(i, (i + 1) % count) for i in range(ends)])  9.43 us
    dot_general x1, matrix products, paired_plan(): pre_partial = jnp.dot(normed, w_expand, preferred_element_type=jnp.float32)  7.8 us
    dot_general x2, matrix products, contract_last(): lax.dot_general(left, right, (((1,), (1,)), ((), ())), preferred_element_...  7.24 us
  transfers between devices with their start and end apart: 13, of which 5 were waited for; matrix products, arithmetic and copies ran while one was open for 12% of the time, Pallas kernels for 14%

profile of v2, /device:TPU:0, one launch (start us, length us, event | category | flops | bytes accessed | tf_op | source)
XLA Modules:
  0.0 297.6 jit_solution(6461789290847903318)
XLA Ops:
  0.7 1.1 fusion.125
  1.8 4.9 %collective-permute-start.1 = (bf16[3,64,192]{2,1,0:T(8,128)(2,1)S(1)}, bf16[3,64,192]{2,1,0:T(8,128)(2,1)S(1)}, u32[]{:S(2)}, u32[]{:S(2)}) collective-permute-start(bf16[3,64,192]{2,1,0:T(8,128)(2,1)S(1)} %get-tuple-element.70), channel_id=1, source_target_pairs={{0,1},{2,3},{4,5},{6,7},{8,9},{10,11},{12,13},{14,15},{16,17},{18,... | collective-permute-start | bytes 221192 | tf_op jit(solution)/shard_map/ppermute | solution.py:22
  6.7 1.3 collective-permute-start.2
  8.0 1.0 slice_convert_fusion.47
  9.0 1.0 slice_convert_fusion.48
  10.0 1.0 fusion.112.block_ref
  11.0 0.9 slice_convert_fusion.46
  11.9 42.0 %gather_plane.2 = bf16[1024,1536]{1,0:T(8,128)(2,1)S(1)} custom-call(bf16[512,192]{1,0:T(8,128)(2,1)S(1)} %fusion.112.block_ref), custom_call_target="tpu_custom_call" | custom-call | tf_op jit(solution)/shard_map/gather_plane/pallas_call | solution.py:295
  53.9 0.1 fusion.116
  54.1 3.8 %add_convert_fusion = bf16[8,64,192]{2,1,0:T(8,128)(2,1)S(1)} fusion(f32[14,70,192]{2,1,0:T(8,128)S(1)} %fusion.116, f32[192]{0:T(256)S(1)} %copy-done.29, f32[192]{0:T(256)S(1)} %bitcast.313, f32[192]{0:T(256)S(1)} %bitcast.315, f32[192]{0:T(256)S(1)} %bitcast.259, f32[192]{0:T(256)S(1)} %bitcast.261, f32[192]{0:T(256)S(1)} %bitcast.263, ...), kind=kLoop, calls=%fused_computation.232 | loop fusion | flops 9732096 | bytes 19502592 | tf_op jit(solution)/shard_map/convert_element_type | solution.py:500
  57.9 40.3 %gather_plane.3 = bf16[1024,1536]{1,0:T(8,128)(2,1)S(1)} custom-call(bf16[512,192]{1,0:T(8,128)(2,1)S(1)} %bitcast.198), custom_call_target="tpu_custom_call" | custom-call | tf_op jit(solution)/shard_map/gather_plane/pallas_call | solution.py:295
  98.2 1.7 copy-done.1
  99.9 1.0 convert_reduce_fusion
  100.9 0.1 collective-permute-start.3
  101.0 4.3 %fusion.127 = (bf16[1024,768]{1,0:T(8,128)(2,1)}, f32[1024,768]{1,0:T(8,128)}) fusion(bf16[1024,1536]{1,0:T(8,128)(2,1)S(1)} %gather_plane.2, bf16[768,1536]{1,0:T(8,128)(2,1)S(1)} %copy-done), kind=kOutput, calls=%fused_computation.311 | convolution fusion | flops 2416705536 | bytes 10223616 | tf_op jit(solution)/shard_map/dot_general | solution.py:64
  105.4 2.0 collective-permute-start
  107.4 0.1 dynamic_slice.17
  107.5 0.1 dynamic_slice.18
  107.6 7.8 %fusion.126 = (bf16[1024,768]{1,0:T(8,128)(2,1)}, f32[1024,768]{1,0:T(8,128)}) fusion(bf16[1536,768]{1,0:T(8,128)(2,1)} %param.16, bf16[1024,1536]{1,0:T(8,128)(2,1)} %copy-done.1, f32[1536]{0:T(1024)S(1)} %dynamic_slice.18, f32[1536]{0:T(1024)S(1)} %dynamic_slice.17, f32[1024]{0:T(1024)S(1)} %add_rsqrt_fusion, f32[1024]{0:T(1024)S(1)} %bitcast.214), kind=kOutput, calls=%fused_computation.310 | convolution fusion | flops 2426142720 | bytes 10244096 | tf_op jit(solution)/shard_map/dot_general | solution.py:511
  115.4 0.1 dynamic_slice.20
  115.5 0.1 dynamic_slice.19
  115.6 27.3 %collective-permute-done = bf16[1024,768]{1,0:T(8,128)(2,1)} collective-permute-done((bf16[1024,768]{1,0:T(8,128)(2,1)}, bf16[1024,768]{1,0:T(8,128)(2,1)}, u32[]{:S(2)}, u32[]{:S(2)}) %collective-permute-start) | collective-permute-done | bytes 1572896 | tf_op jit(solution)/shard_map/ppermute | solution.py:172
  142.9 33.2 %collective-permute-done.4 = bf16[1024,768]{1,0:T(8,128)(2,1)} collective-permute-done((bf16[1024,768]{1,0:T(8,128)(2,1)}, bf16[1024,768]{1,0:T(8,128)(2,1)}, u32[]{:S(2)}, u32[]{:S(2)}) %collective-permute-start.4) | collective-permute-done | bytes 1572896 | tf_op jit(solution)/shard_map/ppermute | solution.py:172
  176.1 4.8 %multiply_convert_fusion = (bf16[1024,768]{1,0:T(8,128)(2,1)S(1)}, bf16[1024,768]{1,0:T(8,128)(2,1)S(1)}) fusion(f32[768]{0:T(1024)S(1)} %copy-done.11, f32[1024,768]{1,0:T(8,128)} %get-tuple-element.126, bf16[1024,768]{1,0:T(8,128)(2,1)} %collective-permute-done.4, f32[1024,768]{1,0:T(8,128)} %get-tuple-element.128, bf16[1024,768]{1,0:T(8,128)(2,1)} %collective-permute-done), kind=kLoop, calls=%fused_computation.66 | loop fusion | flops 14155776 | bytes 12585984 | tf_op jit(solution)/shard_map/convert_element_type | solution.py:515
  180.9 2.8 convolution_convert_fusion.refs_1_
  183.8 2.9 convolution_convert_fusion.1.refs_0_
  186.7 52.8 %scatter_plane.1 = (bf16[512,192]{1,0:T(8,128)(2,1)S(1)}, bf16[512,192]{1,0:T(8,128)(2,1)S(1)}) custom-call(bf16[1024,1536]{1,0:T(8,128)(2,1)S(1)} %convolution_convert_fusion.1.refs_0_, bf16[1024,1536]{1,0:T(8,128)(2,1)S(1)} %convolution_convert_fusion.refs_1_), custom_call_target="tpu_custom_call" | custom-call | tf_op jit(solution)/shard_map/scatter_plane/pallas_call | solution.py:433
  239.5 0.4 fusion.114
  239.9 0.4 collective-permute-start.5
  240.4 0.8 collective-permute-done.5
  241.2 0.6 collective-permute-start.6
  241.8 3.0 %collective-permute-done.6 = f32[2,512]{1,0:T(2,128)S(1)} collective-permute-done((f32[2,512]{1,0:T(2,128)S(1)}, f32[2,512]{1,0:T(2,128)S(1)}, u32[]{:S(2)}, u32[]{:S(2)}) %collective-permute-start.6) | collective-permute-done | bytes 4128 | tf_op jit(solution)/shard_map/ppermute | solution.py:465
  244.9 9.2 %collective-permute-start.7 = (f32[2,512]{1,0:T(2,128)S(1)}, f32[2,512]{1,0:T(2,128)S(1)}, u32[]{:S(2)}, u32[]{:S(2)}) collective-permute-start(f32[2,512]{1,0:T(2,128)S(1)} %fusion.139), channel_id=1, source_target_pairs={{0,8},{2,10},{4,12},{6,14},{8,0},{10,2},{12,4},{14,6},{16,24},{18,... | collective-permute-start | bytes 12296 | tf_op jit(solution)/shard_map/ppermute | solution.py:465
  254.2 5.0 %fusion.120 = f32[1536,768]{1,0:T(8,128)} fusion(bf16[1024,768]{1,0:T(8,128)(2,1)S(1)} %get-tuple-element.65, bf16[1024,1536]{1,0:T(8,128)(2,1)S(1)} %copy-done.2, f32[1536]{0:T(1024)S(1)} %dynamic_slice.18, f32[1536]{0:T(1024)S(1)} %dynamic_slice.17, f32[1024]{0:T(1024)S(1)} %add_rsqrt_fusion, f32[1024]{0:T(1024)S(1)} %bitcast.215), kind=kOutput, calls=%fused_computation.306 | convolution fusion | flops 2425356288 | bytes 9457664 | tf_op jit(solution)/shard_map/dot_general | solution.py:70
  259.2 10.2 %collective-permute-start.8 = (f32[2,512]{1,0:T(2,128)S(1)}, f32[2,512]{1,0:T(2,128)S(1)}, u32[]{:S(2)}, u32[]{:S(2)}) collective-permute-start(f32[2,512]{1,0:T(2,128)S(1)} %add.454), channel_id=1, source_target_pairs={{0,16},{2,18},{4,20},{6,22},{8,24},{10,26},{12,28},{14,30},{16,0},... | collective-permute-start | bytes 12296 | tf_op jit(solution)/shard_map/ppermute | solution.py:465
  269.4 0.9 fusion.113
  270.3 0.7 collective-permute-done.8
  271.0 2.5 fusion.60
  273.5 1.1 fusion.42
  274.7 0.8 fusion.24
  276.0 2.0 collective-permute-start.11
  278.0 1.3 collective-permute-start.10
  279.3 4.6 %collective-permute-start.9 = (bf16[3,64,192]{2,1,0:T(8,128)(2,1)S(1)}, bf16[3,64,192]{2,1,0:T(8,128)(2,1)S(1)}, u32[]{:S(2)}, u32[]{:S(2)}) collective-permute-start(bf16[3,64,192]{2,1,0:T(8,128)(2,1)S(1)} %bitcast.201), channel_id=1, source_target_pairs={{0,1},{2,3},{4,5},{6,7},{8,9},{10,11},{12,13},{14,15},{16,17},{18,... | collective-permute-start | bytes 221192 | tf_op jit(solution)/shard_map/ppermute | solution.py:22
  283.8 7.2 %fusion.128 = f32[768,1536]{1,0:T(8,128)} fusion(bf16[1024,768]{1,0:T(8,128)(2,1)} %copy-done.6, bf16[1024,1536]{1,0:T(8,128)(2,1)} %copy-done.3), kind=kOutput, calls=%fused_computation.312 | convolution fusion | flops 2415919104 | bytes 9437184 | tf_op jit(solution)/shard_map/dot_general | solution.py:70
  291.0 1.2 add.506
  292.3 0.6 add.505
  292.9 0.1 fusion.115
  293.0 4.6 %fusion.63 = bf16[8,64,192]{2,1,0:T(8,128)(2,1)} fusion(f32[14,70,192]{2,1,0:T(8,128)S(1)} %fusion.115, bf16[8,64,192]{2,1,0:T(8,128)(2,1)S(1)} %copy-done.7, f32[192]{0:T(256)S(1)} %bitcast.314, f32[192]{0:T(256)S(1)} %bitcast.316, f32[192]{0:T(256)S(1)} %bitcast.260, f32[192]{0:T(256)S(1)} %bitcast.262, f32[192]{0:T(256)S(1)} %bitcast.264, ...), kind=kLoop, calls=%fused_computation.124 | loop fusion | flops 9830400 | bytes 19698432 | tf_op jit(solution)/shard_map/convert_element_type | solution.py:543
  (99 shorter events, 0.5 us)
Async XLA Ops:
  0.6 100.4 %copy-start = (bf16[768,1536]{1,0:T(8,128)(2,1)S(1)}, bf16[768,1536]{1,0:T(8,128)(2,1)}, u32[]{:S(2)}) copy-start(bf16[768,1536]{1,0:T(8,128)(2,1)} %param.18) | copy-start | bytes 7077892
  0.6 53.2 %copy-start.8 = (bf16[8,64,192]{2,1,0:T(8,128)(2,1)S(1)}, bf16[8,64,192]{2,1,0:T(8,128)(2,1)}, u32[]{:S(2)}) copy-start(bf16[8,64,192]{2,1,0:T(8,128)(2,1)} %param.11) | copy-start | bytes 589828
  0.7 53.4 %copy-start.29 = (f32[192]{0:T(256)S(1)}, f32[192]{0:T(256)}, u32[]{:S(2)}) copy-start(f32[192]{0:T(256)} %param.13) | copy-start | bytes 2308
  1.8 52.1 %collective-permute-start.1 = (bf16[3,64,192]{2,1,0:T(8,128)(2,1)S(1)}, bf16[3,64,192]{2,1,0:T(8,128)(2,1)S(1)}, u32[]{:S(2)}, u32[]{:S(2)}) collective-permute-start(bf16[3,64,192]{2,1,0:T(8,128)(2,1)S(1)} %get-tuple-element.70), channel_id=1, source_target_pairs={{0,1},{2,3},{4,5},{6,7},{8,9},{10,11},{12,13},{14,15},{16,17},{18,... | collective-permute-start | bytes 221192 | tf_op jit(solution)/shard_map/ppermute | solution.py:22
  6.7 47.2 %collective-permute-start.2 = (bf16[3,64,192]{2,1,0:T(8,128)(2,1)S(1)}, bf16[3,64,192]{2,1,0:T(8,128)(2,1)S(1)}, u32[]{:S(2)}, u32[]{:S(2)}) collective-permute-start(bf16[3,64,192]{2,1,0:T(8,128)(2,1)S(1)} %get-tuple-element.71), channel_id=1, source_target_pairs={{1,0},{3,2},{5,4},{7,6},{9,8},{11,10},{13,12},{15,14},{17,16},{19,... | collective-permute-start | bytes 221192 | tf_op jit(solution)/shard_map/ppermute | solution.py:24
  53.9 47.1 %copy-start.3 = (bf16[1024,1536]{1,0:T(8,128)(2,1)}, bf16[1024,1536]{1,0:T(8,128)(2,1)S(1)}, u32[]{:S(2)}) copy-start(bf16[1024,1536]{1,0:T(8,128)(2,1)S(1)} %gather_plane.2) | copy-start | bytes 9437188
  54.0 3.8 %copy-start.4 = (f32[14,70,192]{2,1,0:T(8,128)}, f32[14,70,192]{2,1,0:T(8,128)S(1)}, u32[]{:S(2)}) copy-start(f32[14,70,192]{2,1,0:T(8,128)S(1)} %fusion.116) | copy-start | bytes 2257924
  98.2 1.7 copy-start.1
  100.9 6.5 %copy-start.9 = (f32[3072]{0:T(1024)S(1)}, f32[3072]{0:T(1024)}, u32[]{:S(2)}) copy-start(f32[3072]{0:T(1024)} %param.14) | copy-start | bytes 36868
  100.9 6.5 %copy-start.10 = (f32[3072]{0:T(1024)S(1)}, f32[3072]{0:T(1024)}, u32[]{:S(2)}) copy-start(f32[3072]{0:T(1024)} %param.15) | copy-start | bytes 36868
  100.9 6.6 %collective-permute-start.3 = (f32[2,1024]{1,0:T(2,128)S(1)}, f32[2,1024]{1,0:T(2,128)S(1)}, u32[]{:S(2)}, u32[]{:S(2)}) collective-permute-start(f32[2,1024]{1,0:T(2,128)S(1)} %pad_maximum_fusion), channel_id=1, source_target_pairs={{0,1},{1,0},{2,3},{3,2},{4,5},{5,4},{6,7},{7,6},{8,9},{9,8},{10,11... | collective-permute-start | bytes 24584 | tf_op jit(solution)/shard_map/ppermute | solution.py:172
  105.4 37.5 %collective-permute-start = (bf16[1024,768]{1,0:T(8,128)(2,1)}, bf16[1024,768]{1,0:T(8,128)(2,1)}, u32[]{:S(2)}, u32[]{:S(2)}) collective-permute-start(bf16[1024,768]{1,0:T(8,128)(2,1)} %get-tuple-element.127), channel_id=1, source_target_pairs={{0,1},{1,0},{2,3},{3,2},{4,5},{5,4},{6,7},{7,6},{8,9},{9,8},{10,11... | collective-permute-start | bytes 4718600 | tf_op jit(solution)/shard_map/ppermute | solution.py:172
  107.6 68.5 %copy-start.11 = (f32[768]{0:T(1024)S(1)}, f32[768]{0:T(1024)}, u32[]{:S(2)}) copy-start(f32[768]{0:T(1024)} %param.17) | copy-start | bytes 9220
  115.4 60.7 %collective-permute-start.4 = (bf16[1024,768]{1,0:T(8,128)(2,1)}, bf16[1024,768]{1,0:T(8,128)(2,1)}, u32[]{:S(2)}, u32[]{:S(2)}) collective-permute-start(bf16[1024,768]{1,0:T(8,128)(2,1)} %get-tuple-element.125), channel_id=1, source_target_pairs={{0,1},{1,0},{2,3},{3,2},{4,5},{5,4},{6,7},{7,6},{8,9},{9,8},{10,11... | collective-permute-start | bytes 4718600 | tf_op jit(solution)/shard_map/ppermute | solution.py:172
  180.9 2.9 copy-start.6
  180.9 2.9 copy-start.31
  186.7 67.5 %copy-start.2 = (bf16[1024,1536]{1,0:T(8,128)(2,1)S(1)}, bf16[1024,1536]{1,0:T(8,128)(2,1)}, u32[]{:S(2)}) copy-start(bf16[1024,1536]{1,0:T(8,128)(2,1)} %copy-done.1) | copy-start | bytes 9437188
  239.9 1.2 collective-permute-start.5
  241.2 3.7 %collective-permute-start.6 = (f32[2,512]{1,0:T(2,128)S(1)}, f32[2,512]{1,0:T(2,128)S(1)}, u32[]{:S(2)}, u32[]{:S(2)}) collective-permute-start(f32[2,512]{1,0:T(2,128)S(1)} %fusion.118), channel_id=1, source_target_pairs={{0,4},{2,6},{4,0},{6,2},{8,12},{10,14},{12,8},{14,10},{16,20},{18,... | collective-permute-start | bytes 12296 | tf_op jit(solution)/shard_map/ppermute | solution.py:465
  244.9 24.5 %copy-start.7 = (bf16[8,64,192]{2,1,0:T(8,128)(2,1)S(1)}, bf16[8,64,192]{2,1,0:T(8,128)(2,1)}, u32[]{:S(2)}) copy-start(bf16[8,64,192]{2,1,0:T(8,128)(2,1)} %param.21) | copy-start | bytes 589828
  244.9 24.5 %copy-start.12 = (f32[192]{0:T(256)S(1)}, f32[192]{0:T(256)}, u32[]{:S(2)}) copy-start(f32[192]{0:T(256)} %param.20) | copy-start | bytes 2308
  244.9 24.5 %copy-start.30 = (f32[192]{0:T(256)S(1)}, f32[192]{0:T(256)}, u32[]{:S(2)}) copy-start(f32[192]{0:T(256)} %param.19) | copy-start | bytes 2308
  244.9 14.2 %collective-permute-start.7 = (f32[2,512]{1,0:T(2,128)S(1)}, f32[2,512]{1,0:T(2,128)S(1)}, u32[]{:S(2)}, u32[]{:S(2)}) collective-permute-start(f32[2,512]{1,0:T(2,128)S(1)} %fusion.139), channel_id=1, source_target_pairs={{0,8},{2,10},{4,12},{6,14},{8,0},{10,2},{12,4},{14,6},{16,24},{18,... | collective-permute-start | bytes 12296 | tf_op jit(solution)/shard_map/ppermute | solution.py:465
  259.1 11.8 %copy-start.5 = (f32[14,70,192]{2,1,0:T(8,128)S(1)}, f32[14,70,192]{2,1,0:T(8,128)}, u32[]{:S(2)}) copy-start(f32[14,70,192]{2,1,0:T(8,128)} %copy-done.4) | copy-start | bytes 2257924
  259.2 11.8 %collective-permute-start.8 = (f32[2,512]{1,0:T(2,128)S(1)}, f32[2,512]{1,0:T(2,128)S(1)}, u32[]{:S(2)}, u32[]{:S(2)}) collective-permute-start(f32[2,512]{1,0:T(2,128)S(1)} %add.454), channel_id=1, source_target_pairs={{0,16},{2,18},{4,20},{6,22},{8,24},{10,26},{12,28},{14,30},{16,0},... | collective-permute-start | bytes 12296 | tf_op jit(solution)/shard_map/ppermute | solution.py:465
  270.3 20.8 %collective-permute-start.12 = (f32[192]{0:T(256)S(1)}, f32[192]{0:T(256)}, u32[]{:S(2)}, u32[]{:S(2)}) collective-permute-start(f32[192]{0:T(256)S(1)} %get-tuple-element.66), channel_id=1, source_target_pairs={{0,1},{1,0},{2,3},{3,2},{4,5},{5,4},{6,7},{7,6},{8,9},{9,8},{10,11... | collective-permute-start | bytes 2312 | tf_op jit(solution)/shard_map/ppermute | solution.py:172
  274.6 1.2 copy-start.25
  274.6 1.2 copy-start.26
  274.6 1.2 copy-start.27
  274.6 1.2 copy-start.28
  274.6 1.2 copy-start.18
  274.6 1.2 copy-start.19
  274.6 1.2 copy-start.20
  274.6 1.2 copy-start.21
  274.7 1.2 copy-start.22
  274.7 1.2 copy-start.23
  274.7 1.2 copy-start.24
  274.7 1.3 copy-start.13
  274.7 1.3 copy-start.14
  274.7 1.3 copy-start.15
  274.7 1.3 copy-start.16
  274.7 1.3 copy-start.17
  276.0 16.2 %collective-permute-start.11 = (f32[7,7,192]{2,1,0:T(8,128)S(1)}, f32[7,7,192]{2,1,0:T(8,128)S(1)}, u32[]{:S(2)}, u32[]{:S(2)}) collective-permute-start(f32[7,7,192]{2,1,0:T(8,128)S(1)} %constant_dynamic-update-slice_fusion), channel_id=1, source_target_pairs={{0,1},{1,0},{2,3},{3,2},{4,5},{5,4},{6,7},{7,6},{8,9},{9,8},{10,11... | collective-permute-start | bytes 112904 | tf_op jit(solution)/shard_map/ppermute | solution.py:172
  278.0 14.9 %collective-permute-start.10 = (bf16[3,64,192]{2,1,0:T(8,128)(2,1)S(1)}, bf16[3,64,192]{2,1,0:T(8,128)(2,1)S(1)}, u32[]{:S(2)}, u32[]{:S(2)}) collective-permute-start(bf16[3,64,192]{2,1,0:T(8,128)(2,1)S(1)} %bitcast.202), channel_id=1, source_target_pairs={{1,0},{3,2},{5,4},{7,6},{9,8},{11,10},{13,12},{15,14},{17,16},{19,... | collective-permute-start | bytes 221192 | tf_op jit(solution)/shard_map/ppermute | solution.py:24
  279.3 13.6 %collective-permute-start.9 = (bf16[3,64,192]{2,1,0:T(8,128)(2,1)S(1)}, bf16[3,64,192]{2,1,0:T(8,128)(2,1)S(1)}, u32[]{:S(2)}, u32[]{:S(2)}) collective-permute-start(bf16[3,64,192]{2,1,0:T(8,128)(2,1)S(1)} %bitcast.201), channel_id=1, source_target_pairs={{0,1},{2,3},{4,5},{6,7},{8,9},{10,11},{12,13},{14,15},{16,17},{18,... | collective-permute-start | bytes 221192 | tf_op jit(solution)/shard_map/ppermute | solution.py:22

commit v3 on v2

--- a/solution.py
+++ b/solution.py
@@ -200,10 +200,11 @@
         for peer in peers:
             pl.semaphore_signal(barrier, inc=1, device_id=self.here(peer), device_id_type=MESH)
 
-        pl.semaphore_signal(
-            barrier, inc=1, device_id=(self.trader, 1 - self.row), device_id_type=MESH
-        )
-        pl.semaphore_wait(barrier, len(peers) + 1)
+        for peer in (self.trader, self.tensor):
+            pl.semaphore_signal(
+                barrier, inc=1, device_id=(peer, 1 - self.row), device_id_type=MESH
+            )
+        pl.semaphore_wait(barrier, len(peers) + 2)
 
 
 def remote(source, target, sems, device):
@@ -224,7 +225,9 @@
     return ref.at[rows, pl.ds(pl.multiple_of(panel * width, 128), width)]
 
 
-def gather_kernel(block_ref, out_ref, arrived, block, pre_sem, swap_sem, z_sem, x_sem, c_sem):
+def gather_kernel(paired, *refs):
+    block_ref, out_ref = refs[0], refs[1 + paired]
+    arrived, block, pre_sem, swap_sem, z_sem, x_sem, c_sem, pair_sem = refs[2 + 2 * paired :]
     place = Place()
     quarter = block_ref.shape[0] // 2
     width = block.shape[1]
@@ -235,6 +238,12 @@
     place.meet()
     other_rows = pl.ds(pl.multiple_of((1 - place.core) * quarter, quarter), quarter)
     own_rows = pl.ds(pl.multiple_of(place.core * quarter, quarter), quarter)
+    pair_copies = []
+    if paired:
+        pair_copies.append(
+            remote(refs[1], refs[3], pair_sem, (place.tensor, 1 - place.row))
+        )
+        pair_copies[0].start()
     pairing = remote(block_ref.at[other_rows, :], arrived, pre_sem, place.here(place.sibling))
     pairing.start()
     pairing.wait()
@@ -281,22 +290,24 @@
         chunk = spot(origin)
         c_copies.append(remote(chunk, chunk, c_sem.at[4 + index], place.here(place.sibling)))
         c_copies[-1].start()
-    for copy in c_copies:
+    for copy in c_copies + pair_copies:
         copy.wait_recv()
-    for copy in z_copies + x_copies + c_copies:
+    for copy in pair_copies + z_copies + x_copies + c_copies:
         copy.wait_send()
 
 
-def gather_plane(block, collective_id):
+def gather_plane(block, collective_id, pair=()):
     count = lax.axis_size("tensor")
     positions, channels = block.shape
     quarter, width = positions // 2, 2 * channels
     dma = pltpu.SemaphoreType.DMA
+    vmem = pl.BlockSpec(memory_space=pltpu.VMEM)
+    gathered = jax.ShapeDtypeStruct((2 * positions, count // 2 * channels), block.dtype)
     return pl.pallas_call(
-        gather_kernel,
-        out_shape=jax.ShapeDtypeStruct((2 * positions, count // 2 * channels), block.dtype),
-        in_specs=[pl.BlockSpec(memory_space=pltpu.VMEM)],
-        out_specs=pl.BlockSpec(memory_space=pltpu.VMEM),
+        functools.partial(gather_kernel, len(pair)),
+        out_shape=[gathered] + [jax.ShapeDtypeStruct(p.shape, p.dtype) for p in pair],
+        in_specs=[vmem] * (1 + len(pair)),
+        out_specs=[vmem] * (1 + len(pair)),
         scratch_shapes=[
             pltpu.VMEM((quarter, channels), block.dtype),
             pltpu.VMEM((quarter, width), block.dtype),
@@ -305,12 +316,13 @@
             dma((4, 2)),
             dma((4, 2)),
             dma((8, 2)),
+            dma((2,)),
         ],
         compiler_params=pltpu.CompilerParams(
             collective_id=collective_id, has_side_effects=True, vmem_limit_bytes=24 * 2**20
         ),
         name="gather_plane",
-    )(block)
+    )(block, *pair)
 
 
 def scatter_kernel(arrays, *refs):
@@ -458,13 +470,49 @@
     )(*partials)
 
 
-def butterfly(values):
-    count = lax.axis_size("tensor")
-    step = 1
-    while step < count:
-        values = values + lax.ppermute(values, "tensor", [(i, i ^ step) for i in range(count)])
-        step *= 2
-    return values
+def total_kernel(in_ref, out_ref, held, from_core, from_x, from_z, c_sem, x_sem, z_sem):
+    place = Place()
+    place.meet()
+    c_copy = remote(in_ref, from_core, c_sem, place.here(place.sibling))
+    c_copy.start()
+    c_copy.wait()
+    held[0] = in_ref[...] + from_core[...]
+    x_copy = remote(held.at[0], from_x, x_sem, place.here(place.across))
+    x_copy.start()
+    x_copy.wait()
+    held[1] = held[0] + from_x[...]
+    z_copies = []
+    for step in CHIP_STEPS:
+        copy = remote(
+            held.at[1], from_z.at[step], z_sem.at[step], place.here(place.along(step))
+        )
+        copy.start()
+        z_copies.append(copy)
+    for copy in z_copies:
+        copy.wait()
+    out_ref[...] = held[1] + from_z[1] + from_z[2] + from_z[3]
+
+
+def total_over_tensor(values, collective_id):
+    dma = pltpu.SemaphoreType.DMA
+    vmem = pl.BlockSpec(memory_space=pltpu.VMEM)
+    return pl.pallas_call(
+        total_kernel,
+        out_shape=jax.ShapeDtypeStruct(values.shape, values.dtype),
+        in_specs=[vmem],
+        out_specs=vmem,
+        scratch_shapes=[
+            pltpu.VMEM((2, *values.shape), values.dtype),
+            pltpu.VMEM(values.shape, values.dtype),
+            pltpu.VMEM(values.shape, values.dtype),
+            pltpu.VMEM((4, *values.shape), values.dtype),
+            dma((2,)),
+            dma((2,)),
+            dma((4, 2)),
+        ],
+        compiler_params=pltpu.CompilerParams(collective_id=collective_id, has_side_effects=True),
+        name="total_over_tensor",
+    )(values)
 
 
 def paired_plan(
@@ -493,14 +541,14 @@
     shift_half = lax.dynamic_slice_in_dim(norm_bias, row * half_features, half_features)
     upstream = out_grad.reshape(positions, channels).astype(jnp.float32)
     scaled_grad = (upstream * layer_scale).astype(jnp.bfloat16)
-    grad_panels = gather_plane(scaled_grad, 0)
+    (grad_panels,) = gather_plane(scaled_grad, 0)
     rimmed = extended(image, (("rows", 0),), rim_depth)
     wide_image = jnp.pad(rimmed, ((0, 0), (rim_depth, rim_depth), (0, 0))).astype(jnp.float32)
     convolved = depthwise(wide_image, dw_kernel, height, breadth) + dw_bias
     mixed = convolved.astype(jnp.bfloat16).reshape(positions, channels)
-    mixed_panels = gather_plane(mixed, 1)
     hidden_partial = contract_last(grad_panels, w_project)
-    hidden_grad = hidden_partial + pair_swap(hidden_partial.astype(jnp.bfloat16))
+    mixed_panels, hidden_other = gather_plane(mixed, 1, (hidden_partial.astype(jnp.bfloat16),))
+    hidden_grad = hidden_partial + hidden_other
     mixed_wide = mixed_panels.astype(jnp.float32)
     sums = jnp.stack([jnp.sum(mixed_wide, 1), jnp.sum(mixed_wide * mixed_wide, 1)])
     sums = sums + pair_swap(sums)
@@ -530,7 +578,9 @@
     own_inv_std = lax.dynamic_slice_in_dim(inv_std, row * positions, positions)[:, None]
     centred = (mixed.astype(jnp.float32) - own_average) * own_inv_std
     gain_grad = normed_grad * gain_part
-    totals = butterfly(jnp.stack([jnp.sum(gain_grad, 1), jnp.sum(gain_grad * centred, 1)]))
+    totals = total_over_tensor(
+        jnp.stack([jnp.sum(gain_grad, 1), jnp.sum(gain_grad * centred, 1)]), 3
+    )
     plain_mean = totals[0][:, None] / features
     centred_mean = totals[1][:, None] / features
     mixed_grad = (own_inv_std * (gain_grad - plain_mean - centred * centred_mean)).astype(

time: 298 us -> 289 us (0.970)
  waiting for transfers between devices: 65.1 us -> 34.6 us
  Pallas kernels: 135 us -> 159 us
  starting transfers between devices: 36.6 us -> 17.4 us
  other arithmetic: 25.9 us -> 34.7 us
  local copies, waits for them, and re-layouts: 3.48 us -> 10.1 us
    pallas_call x2 -> x3, Pallas kernels: 82.3 us -> 112 us  [the longest x2 85.8 us: gather_plane(): pl.pallas_call(functools.partial(gather_kernel, len(pair)), out_shape=[ga...]
    ppermute x5 -> x4, waiting for transfers between devices: 60.6 us -> 34.6 us  [pair_swap(): return lax.ppermute(value, 'rows', [(0, 1), (1, 0)])]
    ppermute x4 -> x0, starting transfers between devices: 20.5 us -> none  [butterfly(): lax.ppermute(values, 'tensor', [(i, i ^ step) for i in range(count)])]
    reduce_sum x3, other arithmetic: 4.43 us -> 11.3 us  [kernel_terms(): kernel_line.append(jnp.sum(window * gradient, axis=(0, 1)))]
    pallas_call x1, Pallas kernels: 52.8 us -> 46.8 us  [scatter_plane(): pl.pallas_call(functools.partial(scatter_kernel, arrays), out_shape=[jax....]
    another operation x7, local copies, waits for them, and re-layouts: 0.2 us -> 5.07 us  [kernel_terms(): kernel_rows.append(jnp.stack(kernel_line))]
    ppermute x4 -> x0, waiting for transfers between devices: 4.57 us -> none  [butterfly(): lax.ppermute(values, 'tensor', [(i, i ^ step) for i in range(count)])]
    ppermute x5 -> x4, starting transfers between devices: 4.06 us -> 6.66 us  [pair_swap(): return lax.ppermute(value, 'rows', [(0, 1), (1, 0)])]
  transfers between devices with their start and end apart: 13 -> 8, of which waited for: 5 -> 2; matrix products, arithmetic and copies ran while one was open for 12% -> 8% of each run, Pallas kernels for 14% -> 15%
where the time goes in v3:
time: 289 us; the launch traced here: 288 us
  Pallas kernels  159 us (55%)
  other arithmetic  34.7 us (12%)
  waiting for transfers between devices  34.6 us (12%)
  matrix products  30.1 us (10%)
  starting transfers between devices  17.4 us (6%)
  local copies, waits for them, and re-layouts  10.1 us (3%)
    pallas_call x2, Pallas kernels, gather_plane(): pl.pallas_call(functools.partial(gather_kernel, len(pair)), out_shape=[ga...  85.8 us
    pallas_call x1, Pallas kernels, scatter_plane(): pl.pallas_call(functools.partial(scatter_kernel, arrays), out_shape=[jax....  46.8 us
    ppermute x4, waiting for transfers between devices, pair_swap(): return lax.ppermute(value, 'rows', [(0, 1), (1, 0)])  34.6 us
    pallas_call x1, Pallas kernels, total_over_tensor(): pl.pallas_call(total_kernel, out_shape=jax.ShapeDtypeStruct(values.shape,...  26.3 us
    dot_general x2, matrix products, contract_first(): lax.dot_general(left, right, (((0,), (0,)), ((), ())), preferred_element_...  12.2 us
    reduce_sum x3, other arithmetic, kernel_terms(): kernel_line.append(jnp.sum(window * gradient, axis=(0, 1)))  11.3 us
    ppermute x2, starting transfers between devices, extended(): lax.ppermute(tail, axis, [(i, (i + 1) % count) for i in range(ends)])  8.15 us
    dot_general x1, matrix products, paired_plan(): pre_partial = jnp.dot(normed, w_expand, preferred_element_type=jnp.float32)  7.88 us
  transfers between devices with their start and end apart: 8, of which 2 were waited for; matrix products, arithmetic and copies ran while one was open for 8% of the time, Pallas kernels for 15%

profile of v3, /device:TPU:0, one launch (start us, length us, event | category | flops | bytes accessed | tf_op | source)
XLA Modules:
  0.0 288.1 jit_solution(3581786239561446493)
XLA Ops:
  0.6 1.1 fusion.124
  1.8 4.9 %collective-permute-start = (bf16[3,64,192]{2,1,0:T(8,128)(2,1)S(1)}, bf16[3,64,192]{2,1,0:T(8,128)(2,1)S(1)}, u32[]{:S(2)}, u32[]{:S(2)}) collective-permute-start(bf16[3,64,192]{2,1,0:T(8,128)(2,1)S(1)} %get-tuple-element.74), channel_id=1, source_target_pairs={{0,1},{2,3},{4,5},{6,7},{8,9},{10,11},{12,13},{14,15},{16,17},{18,... | collective-permute-start | bytes 221192 | tf_op jit(solution)/shard_map/ppermute | solution.py:22
  6.6 1.3 collective-permute-start.1
  7.9 1.0 slice_convert_fusion.47
  9.0 1.0 slice_convert_fusion.48
  10.2 1.0 fusion.112.refs_0_
  11.2 42.0 %gather_plane.2 = bf16[1024,1536]{1,0:T(8,128)(2,1)S(1)} custom-call(bf16[512,192]{1,0:T(8,128)(2,1)S(1)} %fusion.112.refs_0_), custom_call_target="tpu_custom_call" | custom-call | tf_op jit(solution)/shard_map/gather_plane/pallas_call | solution.py:306
  53.3 4.3 %fusion.125 = (bf16[1024,768]{1,0:T(8,128)(2,1)S(1)}, f32[1024,768]{1,0:T(8,128)}) fusion(bf16[1024,1536]{1,0:T(8,128)(2,1)S(1)} %gather_plane.2, bf16[768,1536]{1,0:T(8,128)(2,1)S(1)} %copy-done), kind=kOutput, calls=%fused_computation.309 | convolution fusion | flops 2416705536 | bytes 10223616 | tf_op jit(solution)/shard_map/dot_general | solution.py:64
  57.6 0.9 slice_convert_fusion.46
  59.0 3.8 %add_convert_fusion = bf16[8,64,192]{2,1,0:T(8,128)(2,1)S(1)} fusion(f32[14,70,192]{2,1,0:T(8,128)S(1)} %fusion.116, f32[192]{0:T(256)S(1)} %copy-done.91, f32[192]{0:T(256)S(1)} %bitcast.307, f32[192]{0:T(256)S(1)} %bitcast.309, f32[192]{0:T(256)S(1)} %bitcast.253, f32[192]{0:T(256)S(1)} %bitcast.255, f32[192]{0:T(256)S(1)} %bitcast.257, ...), kind=kLoop, calls=%fused_computation.232 | loop fusion | flops 9732096 | bytes 19502592 | tf_op jit(solution)/shard_map/convert_element_type | solution.py:548
  63.0 43.8 %gather_plane.3 = (bf16[1024,1536]{1,0:T(8,128)(2,1)S(1)}, bf16[1024,768]{1,0:T(8,128)(2,1)S(1)}) custom-call(bf16[512,192]{1,0:T(8,128)(2,1)S(1)} %bitcast.198, bf16[1024,768]{1,0:T(8,128)(2,1)S(1)} %get-tuple-element.129.refs_1_), custom_call_target="tpu_custom_call" | custom-call | tf_op jit(solution)/shard_map/gather_plane/pallas_call | solution.py:306
  106.8 1.6 copy-done.2
  108.4 1.0 convert_reduce_fusion
  109.5 2.5 collective-permute-start.2
  112.2 1.5 collective-permute-done.2
  113.7 7.9 %fusion.126 = (bf16[1024,768]{1,0:T(8,128)(2,1)}, f32[1024,768]{1,0:T(8,128)}) fusion(bf16[1536,768]{1,0:T(8,128)(2,1)} %param.16, bf16[1024,1536]{1,0:T(8,128)(2,1)} %copy-done.2, f32[1536]{0:T(1024)S(1)} %dynamic_slice.18, f32[1536]{0:T(1024)S(1)} %dynamic_slice.17, f32[1024]{0:T(1024)S(1)} %add_rsqrt_fusion, f32[1024]{0:T(1024)S(1)} %bitcast.208), kind=kOutput, calls=%fused_computation.310 | convolution fusion | flops 2426142720 | bytes 10244096 | tf_op jit(solution)/shard_map/dot_general | solution.py:559
  121.6 2.0 collective-permute-start.3
  123.8 33.1 %collective-permute-done.3 = bf16[1024,768]{1,0:T(8,128)(2,1)} collective-permute-done((bf16[1024,768]{1,0:T(8,128)(2,1)}, bf16[1024,768]{1,0:T(8,128)(2,1)}, u32[]{:S(2)}, u32[]{:S(2)}) %collective-permute-start.3) | collective-permute-done | bytes 1572896 | tf_op jit(solution)/shard_map/ppermute | solution.py:172
  156.9 4.8 %multiply_convert_fusion = (bf16[1024,768]{1,0:T(8,128)(2,1)S(1)}, bf16[1024,768]{1,0:T(8,128)(2,1)S(1)}) fusion(f32[768]{0:T(1024)S(1)} %copy-done.89, f32[1024,768]{1,0:T(8,128)} %get-tuple-element.132, bf16[1024,768]{1,0:T(8,128)(2,1)} %collective-permute-done.3, f32[1024,768]{1,0:T(8,128)} %get-tuple-element.130, bf16[1024,768]{1,0:T(8,128)(2,1)} %copy-done.4), kind=kLoop, calls=%fused_computation.66 | loop fusion | flops 14155776 | bytes 12585984 | tf_op jit(solution)/shard_map/convert_element_type | solution.py:563
  161.7 2.8 convolution_convert_fusion.refs_1_
  164.6 2.9 %convolution_convert_fusion.1.refs_0_ = bf16[1024,1536]{1,0:T(8,128)(2,1)S(1)} fusion(bf16[1024,768]{1,0:T(8,128)(2,1)S(1)} %get-tuple-element.69, bf16[1536,768]{1,0:T(8,128)(2,1)S(1)} %copy-done.93), kind=kOutput, calls=%fused_computation.59 | convolution fusion | flops 2417491968 | bytes 7077888 | tf_op jit(solution)/shard_map/dot_general | solution.py:64
  167.5 46.8 %scatter_plane.1 = (bf16[512,192]{1,0:T(8,128)(2,1)S(1)}, bf16[512,192]{1,0:T(8,128)(2,1)S(1)}) custom-call(bf16[1024,1536]{1,0:T(8,128)(2,1)S(1)} %convolution_convert_fusion.1.refs_0_, bf16[1024,1536]{1,0:T(8,128)(2,1)S(1)} %convolution_convert_fusion.refs_1_), custom_call_target="tpu_custom_call" | custom-call | tf_op jit(solution)/shard_map/scatter_plane/pallas_call | solution.py:445
  214.7 0.6 pad_maximum_fusion.1.in_ref
  215.3 26.3 %total_over_tensor.1 = f32[2,512]{1,0:T(2,128)} custom-call(f32[2,512]{1,0:T(2,128)} %pad_maximum_fusion.1.in_ref), custom_call_target="tpu_custom_call" | custom-call | tf_op jit(solution)/shard_map/total_over_tensor/pallas_call | solution.py:499
  241.6 0.8 slice_multiply_fusion.52
  242.4 8.2 %fusion.60 = (f32[192]{0:T(256)}, f32[192]{0:T(256)}, f32[192]{0:T(256)}, f32[192]{0:T(256)}, f32[192]{0:T(256)}, /*index=5*/f32[192]{0:T(256)}, f32[192]{0:T(25...) fusion(f32[14,70,192]{2,1,0:T(8,128)} %copy-done.5, ...), kind=kLoop, calls=%fused_computation.120 | loop fusion | flops 4616832 | bytes 7690496 | tf_op jit(solution)/shard_map/reduce_sum | solution.py:58
  250.6 1.7 fusion.42
  252.3 1.4 fusion.24
  253.7 0.5 copy-done.3
  254.2 0.5 copy-done.12
  254.7 5.0 %fusion.119 = f32[1536,768]{1,0:T(8,128)} fusion(bf16[1024,768]{1,0:T(8,128)(2,1)S(1)} %copy-done.12, bf16[1024,1536]{1,0:T(8,128)(2,1)S(1)} %copy-done.3, f32[1536]{0:T(1024)S(1)} %dynamic_slice.18, f32[1536]{0:T(1024)S(1)} %dynamic_slice.17, f32[1024]{0:T(1024)S(1)} %add_rsqrt_fusion, f32[1024]{0:T(1024)S(1)} %bitcast.209), kind=kOutput, calls=%fused_computation.305 | convolution fusion | flops 2425356288 | bytes 9457664 | tf_op jit(solution)/shard_map/dot_general | solution.py:70
  259.7 0.7 fusion.123
  260.3 1.4 fusion.113
  261.8 1.4 collective-permute-start.7
  263.2 0.7 stack.223
  263.9 0.7 stack.232
  264.6 0.7 stack.241
  265.4 0.7 stack.250
  266.1 0.7 stack.259
  266.8 0.7 stack.268
  267.5 0.7 stack.277
  268.3 0.7 collective-permute-start.6
  269.0 3.3 %collective-permute-start.4 = (bf16[3,64,192]{2,1,0:T(8,128)(2,1)}, bf16[3,64,192]{2,1,0:T(8,128)(2,1)S(1)}, u32[]{:S(2)}, u32[]{:S(2)}) collective-permute-start(bf16[3,64,192]{2,1,0:T(8,128)(2,1)} %bitcast.202), channel_id=1, source_target_pairs={{0,1},{2,3},{4,5},{6,7},{8,9},{10,11},{12,13},{14,15},{16,17},{18,... | collective-permute-start | bytes 221192 | tf_op jit(solution)/shard_map/ppermute | solution.py:22
  272.6 1.3 collective-permute-start.5
  273.9 7.2 %fusion.127 = f32[768,1536]{1,0:T(8,128)} fusion(bf16[1024,768]{1,0:T(8,128)(2,1)} %copy-done.7, bf16[1024,1536]{1,0:T(8,128)(2,1)} %copy-done.1), kind=kOutput, calls=%fused_computation.311 | convolution fusion | flops 2415919104 | bytes 9437184 | tf_op jit(solution)/shard_map/dot_general | solution.py:70
  281.1 1.2 add.490
  282.4 0.6 add.489
  283.5 4.6 %fusion.63 = bf16[8,64,192]{2,1,0:T(8,128)(2,1)} fusion(f32[14,70,192]{2,1,0:T(8,128)S(1)} %fusion.115, bf16[8,64,192]{2,1,0:T(8,128)(2,1)S(1)} %copy-done.8, f32[192]{0:T(256)S(1)} %bitcast.308, f32[192]{0:T(256)S(1)} %bitcast.310, f32[192]{0:T(256)S(1)} %bitcast.254, f32[192]{0:T(256)S(1)} %bitcast.256, f32[192]{0:T(256)S(1)} %bitcast.258, ...), kind=kLoop, calls=%fused_computation.124 | loop fusion | flops 9830400 | bytes 19698432 | tf_op jit(solution)/shard_map/convert_element_type | solution.py:593
  (210 shorter events, 1.5 us)
Async XLA Ops:
  0.6 52.6 %copy-start = (bf16[768,1536]{1,0:T(8,128)(2,1)S(1)}, bf16[768,1536]{1,0:T(8,128)(2,1)}, u32[]{:S(2)}) copy-start(bf16[768,1536]{1,0:T(8,128)(2,1)} %param.18) | copy-start | bytes 7077892
  1.8 56.8 %collective-permute-start = (bf16[3,64,192]{2,1,0:T(8,128)(2,1)S(1)}, bf16[3,64,192]{2,1,0:T(8,128)(2,1)S(1)}, u32[]{:S(2)}, u32[]{:S(2)}) collective-permute-start(bf16[3,64,192]{2,1,0:T(8,128)(2,1)S(1)} %get-tuple-element.74), channel_id=1, source_target_pairs={{0,1},{2,3},{4,5},{6,7},{8,9},{10,11},{12,13},{14,15},{16,17},{18,... | collective-permute-start | bytes 221192 | tf_op jit(solution)/shard_map/ppermute | solution.py:22
  6.6 51.9 %collective-permute-start.1 = (bf16[3,64,192]{2,1,0:T(8,128)(2,1)S(1)}, bf16[3,64,192]{2,1,0:T(8,128)(2,1)S(1)}, u32[]{:S(2)}, u32[]{:S(2)}) collective-permute-start(bf16[3,64,192]{2,1,0:T(8,128)(2,1)S(1)} %get-tuple-element.75), channel_id=1, source_target_pairs={{1,0},{3,2},{5,4},{7,6},{9,8},{11,10},{13,12},{15,14},{17,16},{19,... | collective-permute-start | bytes 221192 | tf_op jit(solution)/shard_map/ppermute | solution.py:24
  9.0 49.8 %copy-start.13 = (f32[1,1,192]{2,1,0:T(1,128)}, f32[1,1,192]{2,1,0:T(1,128)S(1)}, u32[]{:S(2)}) copy-start(f32[1,1,192]{2,1,0:T(1,128)S(1)} %get-tuple-element.107) | copy-start | bytes 2308
  9.0 49.8 %copy-start.15 = (f32[1,1,192]{2,1,0:T(1,128)}, f32[1,1,192]{2,1,0:T(1,128)S(1)}, u32[]{:S(2)}) copy-start(f32[1,1,192]{2,1,0:T(1,128)S(1)} %get-tuple-element.108) | copy-start | bytes 2308
  9.0 49.8 %copy-start.17 = (f32[1,1,192]{2,1,0:T(1,128)}, f32[1,1,192]{2,1,0:T(1,128)S(1)}, u32[]{:S(2)}) copy-start(f32[1,1,192]{2,1,0:T(1,128)S(1)} %get-tuple-element.109) | copy-start | bytes 2308
  9.0 49.8 %copy-start.19 = (f32[1,1,192]{2,1,0:T(1,128)}, f32[1,1,192]{2,1,0:T(1,128)S(1)}, u32[]{:S(2)}) copy-start(f32[1,1,192]{2,1,0:T(1,128)S(1)} %get-tuple-element.110) | copy-start | bytes 2308
  9.0 49.8 %copy-start.21 = (f32[1,1,192]{2,1,0:T(1,128)}, f32[1,1,192]{2,1,0:T(1,128)S(1)}, u32[]{:S(2)}) copy-start(f32[1,1,192]{2,1,0:T(1,128)S(1)} %get-tuple-element.111) | copy-start | bytes 2308
  9.0 49.8 %copy-start.23 = (f32[1,1,192]{2,1,0:T(1,128)}, f32[1,1,192]{2,1,0:T(1,128)S(1)}, u32[]{:S(2)}) copy-start(f32[1,1,192]{2,1,0:T(1,128)S(1)} %get-tuple-element.112) | copy-start | bytes 2308
  9.0 49.8 %copy-start.25 = (f32[1,1,192]{2,1,0:T(1,128)}, f32[1,1,192]{2,1,0:T(1,128)S(1)}, u32[]{:S(2)}) copy-start(f32[1,1,192]{2,1,0:T(1,128)S(1)} %get-tuple-element.113) | copy-start | bytes 2308
  10.0 48.8 %copy-start.27 = (f32[1,1,192]{2,1,0:T(1,128)}, f32[1,1,192]{2,1,0:T(1,128)S(1)}, u32[]{:S(2)}) copy-start(f32[1,1,192]{2,1,0:T(1,128)S(1)} %get-tuple-element.76) | copy-start | bytes 2308
  10.0 48.8 %copy-start.29 = (f32[1,1,192]{2,1,0:T(1,128)}, f32[1,1,192]{2,1,0:T(1,128)S(1)}, u32[]{:S(2)}) copy-start(f32[1,1,192]{2,1,0:T(1,128)S(1)} %get-tuple-element.77) | copy-start | bytes 2308
  10.0 48.8 %copy-start.31 = (f32[1,1,192]{2,1,0:T(1,128)}, f32[1,1,192]{2,1,0:T(1,128)S(1)}, u32[]{:S(2)}) copy-start(f32[1,1,192]{2,1,0:T(1,128)S(1)} %get-tuple-element.78) | copy-start | bytes 2308
  10.0 48.8 %copy-start.33 = (f32[1,1,192]{2,1,0:T(1,128)}, f32[1,1,192]{2,1,0:T(1,128)S(1)}, u32[]{:S(2)}) copy-start(f32[1,1,192]{2,1,0:T(1,128)S(1)} %get-tuple-element.79) | copy-start | bytes 2308
  10.1 48.8 %copy-start.35 = (f32[1,1,192]{2,1,0:T(1,128)}, f32[1,1,192]{2,1,0:T(1,128)S(1)}, u32[]{:S(2)}) copy-start(f32[1,1,192]{2,1,0:T(1,128)S(1)} %get-tuple-element.80) | copy-start | bytes 2308
  10.1 48.8 %copy-start.37 = (f32[1,1,192]{2,1,0:T(1,128)}, f32[1,1,192]{2,1,0:T(1,128)S(1)}, u32[]{:S(2)}) copy-start(f32[1,1,192]{2,1,0:T(1,128)S(1)} %get-tuple-element.81) | copy-start | bytes 2308
  10.1 48.8 %copy-start.39 = (f32[1,1,192]{2,1,0:T(1,128)}, f32[1,1,192]{2,1,0:T(1,128)S(1)}, u32[]{:S(2)}) copy-start(f32[1,1,192]{2,1,0:T(1,128)S(1)} %get-tuple-element.82) | copy-start | bytes 2308
  10.1 48.8 %copy-start.41 = (f32[1,1,192]{2,1,0:T(1,128)}, f32[1,1,192]{2,1,0:T(1,128)S(1)}, u32[]{:S(2)}) copy-start(f32[1,1,192]{2,1,0:T(1,128)S(1)} %get-tuple-element.83) | copy-start | bytes 2308
  10.1 48.8 %copy-start.43 = (f32[1,1,192]{2,1,0:T(1,128)}, f32[1,1,192]{2,1,0:T(1,128)S(1)}, u32[]{:S(2)}) copy-start(f32[1,1,192]{2,1,0:T(1,128)S(1)} %get-tuple-element.84) | copy-start | bytes 2308
  10.1 48.8 %copy-start.45 = (f32[1,1,192]{2,1,0:T(1,128)}, f32[1,1,192]{2,1,0:T(1,128)S(1)}, u32[]{:S(2)}) copy-start(f32[1,1,192]{2,1,0:T(1,128)S(1)} %get-tuple-element.85) | copy-start | bytes 2308
  10.1 48.8 %copy-start.47 = (f32[1,1,192]{2,1,0:T(1,128)}, f32[1,1,192]{2,1,0:T(1,128)S(1)}, u32[]{:S(2)}) copy-start(f32[1,1,192]{2,1,0:T(1,128)S(1)} %get-tuple-element.86) | copy-start | bytes 2308
  10.1 48.8 %copy-start.49 = (f32[1,1,192]{2,1,0:T(1,128)}, f32[1,1,192]{2,1,0:T(1,128)S(1)}, u32[]{:S(2)}) copy-start(f32[1,1,192]{2,1,0:T(1,128)S(1)} %get-tuple-element.87) | copy-start | bytes 2308
  10.1 48.8 %copy-start.51 = (f32[1,1,192]{2,1,0:T(1,128)}, f32[1,1,192]{2,1,0:T(1,128)S(1)}, u32[]{:S(2)}) copy-start(f32[1,1,192]{2,1,0:T(1,128)S(1)} %get-tuple-element.88) | copy-start | bytes 2308
  10.1 48.8 %copy-start.53 = (f32[1,1,192]{2,1,0:T(1,128)}, f32[1,1,192]{2,1,0:T(1,128)S(1)}, u32[]{:S(2)}) copy-start(f32[1,1,192]{2,1,0:T(1,128)S(1)} %get-tuple-element.89) | copy-start | bytes 2308
  10.2 48.8 %copy-start.55 = (f32[1,1,192]{2,1,0:T(1,128)}, f32[1,1,192]{2,1,0:T(1,128)S(1)}, u32[]{:S(2)}) copy-start(f32[1,1,192]{2,1,0:T(1,128)S(1)} %get-tuple-element.90) | copy-start | bytes 2308
  10.2 48.8 %copy-start.57 = (f32[1,1,192]{2,1,0:T(1,128)}, f32[1,1,192]{2,1,0:T(1,128)S(1)}, u32[]{:S(2)}) copy-start(f32[1,1,192]{2,1,0:T(1,128)S(1)} %get-tuple-element.91) | copy-start | bytes 2308
  10.2 48.8 %copy-start.59 = (f32[1,1,192]{2,1,0:T(1,128)}, f32[1,1,192]{2,1,0:T(1,128)S(1)}, u32[]{:S(2)}) copy-start(f32[1,1,192]{2,1,0:T(1,128)S(1)} %get-tuple-element.92) | copy-start | bytes 2308
  10.2 48.8 %copy-start.61 = (f32[1,1,192]{2,1,0:T(1,128)}, f32[1,1,192]{2,1,0:T(1,128)S(1)}, u32[]{:S(2)}) copy-start(f32[1,1,192]{2,1,0:T(1,128)S(1)} %get-tuple-element.93) | copy-start | bytes 2308
  10.2 48.8 %copy-start.63 = (f32[1,1,192]{2,1,0:T(1,128)}, f32[1,1,192]{2,1,0:T(1,128)S(1)}, u32[]{:S(2)}) copy-start(f32[1,1,192]{2,1,0:T(1,128)S(1)} %get-tuple-element.94) | copy-start | bytes 2308
  62.9 49.1 %copy-start.87 = (f32[3072]{0:T(1024)S(1)}, f32[3072]{0:T(1024)}, u32[]{:S(2)}) copy-start(f32[3072]{0:T(1024)} %param.14) | copy-start | bytes 36868
  63.0 49.2 %copy-start.88 = (f32[3072]{0:T(1024)S(1)}, f32[3072]{0:T(1024)}, u32[]{:S(2)}) copy-start(f32[3072]{0:T(1024)} %param.15) | copy-start | bytes 36868
  109.5 4.2 %collective-permute-start.2 = (f32[2,1024]{1,0:T(2,128)S(1)}, f32[2,1024]{1,0:T(2,128)S(1)}, u32[]{:S(2)}, u32[]{:S(2)}) collective-permute-start(f32[2,1024]{1,0:T(2,128)S(1)} %pad_maximum_fusion), channel_id=1, source_target_pairs={{0,1},{1,0},{2,3},{3,2},{4,5},{5,4},{6,7},{7,6},{8,9},{9,8},{10,11... | collective-permute-start | bytes 24584 | tf_op jit(solution)/shard_map/ppermute | solution.py:172
  113.7 43.2 %copy-start.89 = (f32[768]{0:T(1024)S(1)}, f32[768]{0:T(1024)}, u32[]{:S(2)}) copy-start(f32[768]{0:T(1024)} %param.17) | copy-start | bytes 9220
  121.6 35.3 %collective-permute-start.3 = (bf16[1024,768]{1,0:T(8,128)(2,1)}, bf16[1024,768]{1,0:T(8,128)(2,1)}, u32[]{:S(2)}, u32[]{:S(2)}) collective-permute-start(bf16[1024,768]{1,0:T(8,128)(2,1)} %get-tuple-element.131), channel_id=1, source_target_pairs={{0,1},{1,0},{2,3},{3,2},{4,5},{5,4},{6,7},{7,6},{8,9},{9,8},{10,11... | collective-permute-start | bytes 4718600 | tf_op jit(solution)/shard_map/ppermute | solution.py:172
  261.8 19.4 %collective-permute-start.7 = (f32[192]{0:T(256)}, f32[192]{0:T(256)S(1)}, u32[]{:S(2)}, u32[]{:S(2)}) collective-permute-start(f32[192]{0:T(256)} %get-tuple-element.70), channel_id=1, source_target_pairs={{0,1},{1,0},{2,3},{3,2},{4,5},{5,4},{6,7},{7,6},{8,9},{9,8},{10,11... | collective-permute-start | bytes 2312 | tf_op jit(solution)/shard_map/ppermute | solution.py:172
  268.3 14.1 %collective-permute-start.6 = (f32[7,7,192]{2,1,0:T(8,128)S(1)}, f32[7,7,192]{2,1,0:T(8,128)S(1)}, u32[]{:S(2)}, u32[]{:S(2)}) collective-permute-start(f32[7,7,192]{2,1,0:T(8,128)S(1)} %constant_dynamic-update-slice_fusion), channel_id=1, source_target_pairs={{0,1},{1,0},{2,3},{3,2},{4,5},{5,4},{6,7},{7,6},{8,9},{9,8},{10,11... | collective-permute-start | bytes 112904 | tf_op jit(solution)/shard_map/ppermute | solution.py:172
  269.0 14.0 %collective-permute-start.4 = (bf16[3,64,192]{2,1,0:T(8,128)(2,1)}, bf16[3,64,192]{2,1,0:T(8,128)(2,1)S(1)}, u32[]{:S(2)}, u32[]{:S(2)}) collective-permute-start(bf16[3,64,192]{2,1,0:T(8,128)(2,1)} %bitcast.202), channel_id=1, source_target_pairs={{0,1},{2,3},{4,5},{6,7},{8,9},{10,11},{12,13},{14,15},{16,17},{18,... | collective-permute-start | bytes 221192 | tf_op jit(solution)/shard_map/ppermute | solution.py:22
  272.3 10.9 %copy-start.14 = (f32[1,1,192]{2,1,0:T(1,128)S(1)}, f32[1,1,192]{2,1,0:T(1,128)}, u32[]{:S(2)}) copy-start(f32[1,1,192]{2,1,0:T(1,128)} %copy-done.13) | copy-start | bytes 2308
  272.3 10.9 %copy-start.16 = (f32[1,1,192]{2,1,0:T(1,128)S(1)}, f32[1,1,192]{2,1,0:T(1,128)}, u32[]{:S(2)}) copy-start(f32[1,1,192]{2,1,0:T(1,128)} %copy-done.15) | copy-start | bytes 2308
  272.3 10.9 %copy-start.18 = (f32[1,1,192]{2,1,0:T(1,128)S(1)}, f32[1,1,192]{2,1,0:T(1,128)}, u32[]{:S(2)}) copy-start(f32[1,1,192]{2,1,0:T(1,128)} %copy-done.17) | copy-start | bytes 2308
  272.3 10.9 %copy-start.20 = (f32[1,1,192]{2,1,0:T(1,128)S(1)}, f32[1,1,192]{2,1,0:T(1,128)}, u32[]{:S(2)}) copy-start(f32[1,1,192]{2,1,0:T(1,128)} %copy-done.19) | copy-start | bytes 2308
  272.3 10.9 %copy-start.22 = (f32[1,1,192]{2,1,0:T(1,128)S(1)}, f32[1,1,192]{2,1,0:T(1,128)}, u32[]{:S(2)}) copy-start(f32[1,1,192]{2,1,0:T(1,128)} %copy-done.21) | copy-start | bytes 2308
  272.3 10.9 %copy-start.24 = (f32[1,1,192]{2,1,0:T(1,128)S(1)}, f32[1,1,192]{2,1,0:T(1,128)}, u32[]{:S(2)}) copy-start(f32[1,1,192]{2,1,0:T(1,128)} %copy-done.23) | copy-start | bytes 2308
  272.3 10.9 %copy-start.26 = (f32[1,1,192]{2,1,0:T(1,128)S(1)}, f32[1,1,192]{2,1,0:T(1,128)}, u32[]{:S(2)}) copy-start(f32[1,1,192]{2,1,0:T(1,128)} %copy-done.25) | copy-start | bytes 2308
  272.3 10.9 %copy-start.28 = (f32[1,1,192]{2,1,0:T(1,128)S(1)}, f32[1,1,192]{2,1,0:T(1,128)}, u32[]{:S(2)}) copy-start(f32[1,1,192]{2,1,0:T(1,128)} %copy-done.27) | copy-start | bytes 2308
  272.4 10.9 %copy-start.30 = (f32[1,1,192]{2,1,0:T(1,128)S(1)}, f32[1,1,192]{2,1,0:T(1,128)}, u32[]{:S(2)}) copy-start(f32[1,1,192]{2,1,0:T(1,128)} %copy-done.29) | copy-start | bytes 2308
  272.4 10.9 %copy-start.32 = (f32[1,1,192]{2,1,0:T(1,128)S(1)}, f32[1,1,192]{2,1,0:T(1,128)}, u32[]{:S(2)}) copy-start(f32[1,1,192]{2,1,0:T(1,128)} %copy-done.31) | copy-start | bytes 2308
  272.6 10.4 %collective-permute-start.5 = (bf16[3,64,192]{2,1,0:T(8,128)(2,1)S(1)}, bf16[3,64,192]{2,1,0:T(8,128)(2,1)S(1)}, u32[]{:S(2)}, u32[]{:S(2)}) collective-permute-start(bf16[3,64,192]{2,1,0:T(8,128)(2,1)S(1)} %bitcast.201), channel_id=1, source_target_pairs={{1,0},{3,2},{5,4},{7,6},{9,8},{11,10},{13,12},{15,14},{17,16},{19,... | collective-permute-start | bytes 221192 | tf_op jit(solution)/shard_map/ppermute | solution.py:24
  (54 other events, 409.9 us)
